TPU v7x, 256 devices: a whole 4x4x8 slice. The times are simulated.
256 devices in a mesh: rows: 16 (over z_lo, x, core), cols: 16 (over z_hi, y).
Axes of the slice: x: 4, y: 4, z: 8 (z_hi: 4, z_lo: 2; z = z_hi * 2 + z_lo), core: 2. Of those that a mesh axis runs over, the one named last changes fastest.
Arguments:
- search_vectors: bfloat16 [16384, 1024], P(('rows', 'cols')), may hold values from -6 to 6
- tile_values: bfloat16 [256, 64, 512], P('rows'), may hold values from -0.25 to 0.25
- block_columns: int32 [256, 8], P('rows'), may hold values from -4 to 259, as said below
Outputs:
- filtered: bfloat16 [16384, 1024], P(('rows', 'cols'))
- gram: float32 [1024, 1024], P('cols')
Inputs may be any that keep to these rules, and one draw needn't show every extreme that they name: `block_columns`: row b names 8 distinct block columns, each within 4 of b, always including b - 4, b and b + 4; block columns outside 0 to 255 stand for zero tiles.
All inputs are finite; a program needn't handle non-finite values.
Results may differ from a plain program's by a relative error of at most 0.023.
Values may be sent and summed in bfloat16 or wider, within the bound.
A program may use at most 64 MiB of HBM per device.

v0:
```python
import jax
import jax.numpy as jnp
from jax import lax
from jax.sharding import PartitionSpec as P

HALO = 4
DEGREE = 8


shift_value = 0.1
half_width = 2.0


def extended(shard, sides, width):
    for axis, dim in sides:
        size, length = (lax.axis_size(axis), shard.shape[dim])
        up = [(i, (i + 1) % size) for i in range(size - 1)]
        down = [(j, i) for i, j in up]
        last = lax.slice_in_dim(shard, length - width, length, axis=dim)
        first = lax.slice_in_dim(shard, 0, width, axis=dim)
        before = lax.ppermute(last, axis, up)
        after = lax.ppermute(first, axis, down)
        shard = jnp.concatenate([before, shard, after], axis=dim)
    return shard


def per_device(search_vectors, tile_values, block_columns):
    group_count = lax.axis_size("cols")
    row_part = lax.axis_index("rows")
    block_rows = tile_values.shape[0]
    tile_size = tile_values.shape[1]
    tile_count = block_columns.shape[1]
    columns = lax.all_to_all(search_vectors, "cols", split_axis=1, concat_axis=0, tiled=True)
    anchors = row_part * block_rows + jnp.arange(block_rows, dtype=jnp.int32)
    offsets = block_columns - anchors[:, None]
    split_tiles = tile_values.reshape(block_rows, tile_size, tile_count, tile_size)
    band_list = []
    for offset in range(-HALO, HALO + 1):
        selector = (offsets == offset).astype(jnp.float32)
        placed = jnp.einsum("bk,bikj->bij", selector, split_tiles.astype(jnp.float32))
        band_list.append(placed.astype(jnp.bfloat16))

    def filter_step(iterate):
        rounded = iterate.astype(jnp.bfloat16)
        padded = extended(rounded, (("rows", 0),), HALO * tile_size)
        stacked = padded.reshape(block_rows + 2 * HALO, tile_size, rounded.shape[1])
        product = jnp.zeros((block_rows, tile_size, rounded.shape[1]), jnp.float32)
        for position in range(2 * HALO + 1):
            window = lax.slice_in_dim(stacked, position, position + block_rows, axis=0)
            product = product + jnp.einsum(
                "bij,bjc->bic", band_list[position], window, preferred_element_type=jnp.float32
            )
        return (product.reshape(iterate.shape) - shift_value * iterate) / half_width

    previous = columns.astype(jnp.float32)
    current = filter_step(previous)
    for degree_step in range(DEGREE - 1):
        following = 2.0 * filter_step(current) - previous
        previous, current = (current, following)
    filtered = current.astype(jnp.bfloat16)
    rowwise = lax.all_to_all(filtered, "cols", split_axis=0, concat_axis=1, tiled=True)
    width = rowwise.shape[1]
    share_rows = width // group_count
    total_rows = block_rows * tile_size * lax.axis_size("rows")
    partial_value = lax.dot_general(
        rowwise, rowwise, (((0,), (0,)), ((), ())), preferred_element_type=jnp.float32
    )
    group_sum = lax.psum(partial_value.astype(jnp.bfloat16), "cols")
    summed = lax.psum(group_sum, "rows").astype(jnp.float32)
    gram = lax.dynamic_slice_in_dim(summed, lax.axis_index("cols") * share_rows, share_rows, 0)
    return (rowwise, gram * (1.0 / total_rows))


def solution(mesh):
    return jax.shard_map(
        per_device,
        mesh=mesh,
        in_specs=(P(("rows", "cols"), None), P("rows", None, None), P("rows", None)),
        out_specs=(P(("rows", "cols"), None), P("cols", None)),
        check_vma=False,
    )
```

profile of v0, /device:TPU:1, one launch (start us, length us, event | category | flops | bytes accessed | tf_op | source)
XLA Modules:
  0.0 463.5 jit_solution(16485383476500412947)
XLA Ops:
  7.2 1.2 all_to_all.26
  9.4 11.7 %all-to-all-start = ((bf16[16,2,2048]{2,1,0:T(2,128)(2,1)}), bf16[16,2,2048]{2,1,0:T(2,128)(2,1)S(1)}, u32[]{:S(2)}, u32[]{:S(2)}) async-start(bf16[16,2,2048]{2,1,0:T(2,128)(2,1)} %reshape.148), calls=%async_computation | async-start | bytes 262144 | tf_op jit(solution)/shard_map/all_to_all | solution.py:33
  21.2 1.3 compare_bitcast_fusion
  34.2 4.0 collective-permute-start
  38.1 1.9 collective-permute-start.1
  40.3 3.4 collective-permute-done.1
  46.7 1.9 collective-permute-start.2
  48.7 2.6 collective-permute-start.3
  51.5 2.7 collective-permute-done.3
  56.5 1.9 collective-permute-start.4
  58.4 2.4 collective-permute-start.5
  61.1 2.9 collective-permute-done.5
  66.4 1.9 collective-permute-start.6
  68.4 2.4 collective-permute-start.7
  71.0 3.8 collective-permute-done.7
  77.2 1.9 collective-permute-start.8
  79.1 2.4 collective-permute-start.9
  81.8 5.1 %collective-permute-done.9 = bf16[256,64]{1,0:T(8,128)(2,1)S(1)} collective-permute-done((bf16[256,64]{1,0:T(8,128)(2,1)S(1)}, bf16[256,64]{1,0:T(8,128)(2,1)S(1)}, u32[]{:S(2)}, u32[]{:S(2)}) %collective-permute-start.9) | collective-permute-done | bytes 32800 | tf_op jit(solution)/shard_map/ppermute | solution.py:22
  89.1 1.9 collective-permute-start.10
  91.0 2.4 collective-permute-start.11
  93.6 5.1 %collective-permute-done.11 = bf16[256,64]{1,0:T(8,128)(2,1)S(1)} collective-permute-done((bf16[256,64]{1,0:T(8,128)(2,1)S(1)}, bf16[256,64]{1,0:T(8,128)(2,1)S(1)}, u32[]{:S(2)}, u32[]{:S(2)}) %collective-permute-start.11) | collective-permute-done | bytes 32800 | tf_op jit(solution)/shard_map/ppermute | solution.py:22
  100.9 1.9 collective-permute-start.12
  102.9 2.4 collective-permute-start.13
  105.6 5.0 %collective-permute-done.13 = bf16[256,64]{1,0:T(8,128)(2,1)S(1)} collective-permute-done((bf16[256,64]{1,0:T(8,128)(2,1)S(1)}, bf16[256,64]{1,0:T(8,128)(2,1)S(1)}, u32[]{:S(2)}, u32[]{:S(2)}) %collective-permute-start.13) | collective-permute-done | bytes 32800 | tf_op jit(solution)/shard_map/ppermute | solution.py:22
  112.9 1.9 collective-permute-start.14
  114.8 2.6 collective-permute-start.15
  117.7 4.8 %collective-permute-done.15 = bf16[256,64]{1,0:T(8,128)(2,1)S(1)} collective-permute-done((bf16[256,64]{1,0:T(8,128)(2,1)S(1)}, bf16[256,64]{1,0:T(8,128)(2,1)S(1)}, u32[]{:S(2)}, u32[]{:S(2)}) %collective-permute-start.15) | collective-permute-done | bytes 32800 | tf_op jit(solution)/shard_map/ppermute | solution.py:22
  124.9 18.4 %all_to_all.35 = bf16[16,2,2048]{2,1,0:T(2,128)(2,1)S(1)} all-to-all(bf16[16,2,2048]{2,1,0:T(2,128)(2,1)S(1)} %reshape.150), channel_id=1, replica_groups=mesh['rows'=16,'cols'=16] {'cols'}, dimensions={0} | all-to-all | bytes 262144 | tf_op jit(solution)/shard_map/all_to_all | solution.py:61
  143.9 2.1 convolution_convert_fusion
  146.1 170.6 %all-reduce.3.cloned.1.call-done = bf16[1024,1024]{1,0:T(8,128)(2,1)} async-done(((bf16[1024,1024]{1,0:T(8,128)(2,1)}), bf16[1024,1024]{1,0:T(8,128)(2,1)}) %all-reduce.3.cloned.1.call-update) | async-done | bytes 2097168 | tf_op jit(solution)/shard_map/psum | solution.py:68
  316.7 138.3 %all-reduce.5.cloned.1.call-done = bf16[1024,1024]{1,0:T(8,128)(2,1)} async-done(((bf16[1024,1024]{1,0:T(8,128)(2,1)}), bf16[1024,1024]{1,0:T(8,128)(2,1)}) %all-reduce.5.cloned.1.call-update) | async-done | bytes 2097168 | tf_op jit(solution)/shard_map/psum | solution.py:69
  455.0 1.6 convert_multiply_fusion.2
  (155 shorter events, 33.9 us)
Async XLA Ops:
  7.2 15.4 %copy-start.4 = (bf16[16,64,512]{2,1,0:T(8,128)(2,1)S(1)}, bf16[16,64,512]{2,1,0:T(8,128)(2,1)}, u32[]{:S(2)}) copy-start(bf16[16,64,512]{2,1,0:T(8,128)(2,1)} %param.4) | copy-start | bytes 3145732
  9.4 24.5 %all-to-all-start = ((bf16[16,2,2048]{2,1,0:T(2,128)(2,1)}), bf16[16,2,2048]{2,1,0:T(2,128)(2,1)S(1)}, u32[]{:S(2)}, u32[]{:S(2)}) async-start(bf16[16,2,2048]{2,1,0:T(2,128)(2,1)} %reshape.148), calls=%async_computation | async-start | bytes 262144 | tf_op jit(solution)/shard_map/all_to_all | solution.py:33
  21.1 295.5 %all-reduce.3.cloned.1.call-start = ((), (), s32[]{:S(2)}) async-start(), calls=%async_computation.2 | async-start | bytes 4194304 | tf_op jit(solution)/shard_map/psum | solution.py:68
  34.2 6.1 %collective-permute-start = (bf16[256,64]{1,0:T(8,128)(2,1)S(1)}, bf16[256,64]{1,0:T(8,128)(2,1)S(1)}, u32[]{:S(2)}, u32[]{:S(2)}) collective-permute-start(bf16[256,64]{1,0:T(8,128)(2,1)S(1)} %bitcast.451), channel_id=1, source_target_pairs={{0,16},{16,32},{32,48},{48,64},{64,80},{80,96},{96,112},{112,128},... | collective-permute-start | bytes 98312 | tf_op jit(solution)/shard_map/ppermute | solution.py:21
  38.1 5.6 %collective-permute-start.1 = (bf16[256,64]{1,0:T(8,128)(2,1)S(1)}, bf16[256,64]{1,0:T(8,128)(2,1)S(1)}, u32[]{:S(2)}, u32[]{:S(2)}) collective-permute-start(bf16[256,64]{1,0:T(8,128)(2,1)S(1)} %bitcast.450), channel_id=1, source_target_pairs={{16,0},{32,16},{48,32},{64,48},{80,64},{96,80},{112,96},{128,112},... | collective-permute-start | bytes 98312 | tf_op jit(solution)/shard_map/ppermute | solution.py:22
  44.0 1.0 copy-start.2
  44.7 1.0 copy-start
  45.2 1.0 copy-start.1
  46.7 4.8 %collective-permute-start.2 = (bf16[256,64]{1,0:T(8,128)(2,1)S(1)}, bf16[256,64]{1,0:T(8,128)(2,1)S(1)}, u32[]{:S(2)}, u32[]{:S(2)}) collective-permute-start(bf16[256,64]{1,0:T(8,128)(2,1)S(1)} %get-tuple-element.111), channel_id=1, source_target_pairs={{0,16},{16,32},{32,48},{48,64},{64,80},{80,96},{96,112},{112,128},... | collective-permute-start | bytes 98312 | tf_op jit(solution)/shard_map/ppermute | solution.py:21
  48.7 5.6 %collective-permute-start.3 = (bf16[256,64]{1,0:T(8,128)(2,1)S(1)}, bf16[256,64]{1,0:T(8,128)(2,1)S(1)}, u32[]{:S(2)}, u32[]{:S(2)}) collective-permute-start(bf16[256,64]{1,0:T(8,128)(2,1)S(1)} %get-tuple-element.110), channel_id=1, source_target_pairs={{16,0},{32,16},{48,32},{64,48},{80,64},{96,80},{112,96},{128,112},... | collective-permute-start | bytes 98312 | tf_op jit(solution)/shard_map/ppermute | solution.py:22
  56.5 4.6 collective-permute-start.4
  58.4 5.6 %collective-permute-start.5 = (bf16[256,64]{1,0:T(8,128)(2,1)S(1)}, bf16[256,64]{1,0:T(8,128)(2,1)S(1)}, u32[]{:S(2)}, u32[]{:S(2)}) collective-permute-start(bf16[256,64]{1,0:T(8,128)(2,1)S(1)} %get-tuple-element.104), channel_id=1, source_target_pairs={{16,0},{32,16},{48,32},{64,48},{80,64},{96,80},{112,96},{128,112},... | collective-permute-start | bytes 98312 | tf_op jit(solution)/shard_map/ppermute | solution.py:22
  66.4 4.6 collective-permute-start.6
  68.4 6.4 %collective-permute-start.7 = (bf16[256,64]{1,0:T(8,128)(2,1)S(1)}, bf16[256,64]{1,0:T(8,128)(2,1)S(1)}, u32[]{:S(2)}, u32[]{:S(2)}) collective-permute-start(bf16[256,64]{1,0:T(8,128)(2,1)S(1)} %get-tuple-element.98), channel_id=1, source_target_pairs={{16,0},{32,16},{48,32},{64,48},{80,64},{96,80},{112,96},{128,112},... | collective-permute-start | bytes 98312 | tf_op jit(solution)/shard_map/ppermute | solution.py:22
  77.2 4.6 collective-permute-start.8
  79.1 7.7 %collective-permute-start.9 = (bf16[256,64]{1,0:T(8,128)(2,1)S(1)}, bf16[256,64]{1,0:T(8,128)(2,1)S(1)}, u32[]{:S(2)}, u32[]{:S(2)}) collective-permute-start(bf16[256,64]{1,0:T(8,128)(2,1)S(1)} %get-tuple-element.92), channel_id=1, source_target_pairs={{16,0},{32,16},{48,32},{64,48},{80,64},{96,80},{112,96},{128,112},... | collective-permute-start | bytes 98312 | tf_op jit(solution)/shard_map/ppermute | solution.py:22
  89.1 4.6 collective-permute-start.10
  91.0 7.7 %collective-permute-start.11 = (bf16[256,64]{1,0:T(8,128)(2,1)S(1)}, bf16[256,64]{1,0:T(8,128)(2,1)S(1)}, u32[]{:S(2)}, u32[]{:S(2)}) collective-permute-start(bf16[256,64]{1,0:T(8,128)(2,1)S(1)} %get-tuple-element.86), channel_id=1, source_target_pairs={{16,0},{32,16},{48,32},{64,48},{80,64},{96,80},{112,96},{128,112},... | collective-permute-start | bytes 98312 | tf_op jit(solution)/shard_map/ppermute | solution.py:22
  100.9 4.6 collective-permute-start.12
  102.9 7.7 %collective-permute-start.13 = (bf16[256,64]{1,0:T(8,128)(2,1)S(1)}, bf16[256,64]{1,0:T(8,128)(2,1)S(1)}, u32[]{:S(2)}, u32[]{:S(2)}) collective-permute-start(bf16[256,64]{1,0:T(8,128)(2,1)S(1)} %get-tuple-element.80), channel_id=1, source_target_pairs={{16,0},{32,16},{48,32},{64,48},{80,64},{96,80},{112,96},{128,112},... | collective-permute-start | bytes 98312 | tf_op jit(solution)/shard_map/ppermute | solution.py:22
  112.9 4.9 %collective-permute-start.14 = (bf16[256,64]{1,0:T(8,128)(2,1)S(1)}, bf16[256,64]{1,0:T(8,128)(2,1)S(1)}, u32[]{:S(2)}, u32[]{:S(2)}) collective-permute-start(bf16[256,64]{1,0:T(8,128)(2,1)S(1)} %get-tuple-element.75), channel_id=1, source_target_pairs={{0,16},{16,32},{32,48},{48,64},{64,80},{80,96},{96,112},{112,128},... | collective-permute-start | bytes 98312 | tf_op jit(solution)/shard_map/ppermute | solution.py:21
  114.8 7.7 %collective-permute-start.15 = (bf16[256,64]{1,0:T(8,128)(2,1)S(1)}, bf16[256,64]{1,0:T(8,128)(2,1)S(1)}, u32[]{:S(2)}, u32[]{:S(2)}) collective-permute-start(bf16[256,64]{1,0:T(8,128)(2,1)S(1)} %get-tuple-element.74), channel_id=1, source_target_pairs={{16,0},{32,16},{48,32},{64,48},{80,64},{96,80},{112,96},{128,112},... | collective-permute-start | bytes 98312 | tf_op jit(solution)/shard_map/ppermute | solution.py:22
  143.9 2.1 copy-start.3
  146.0 309.0 %all-reduce.5.cloned.1.call-start = ((), (), s32[]{:S(2)}) async-start(), calls=%async_computation.3 | async-start | bytes 4194304 | tf_op jit(solution)/shard_map/psum | solution.py:69
Sparse Core Ops, SparseCore 0:
  146.1 170.4 all-reduce.2
  319.3 135.6 all-reduce.4
where the time goes:
time: 464 us
  waiting for transfers between devices  342 us (74%)
  starting transfers between devices  48.4 us (10%)
  matrix products  24.5 us (5%)
  blocking collectives  18.4 us (4%)
  between operations  15 us (3%)
  other arithmetic  8.8 us (2%)
  local copies, waits for them, and re-layouts  6.7 us (1%)
    psum x1, waiting for transfers between devices, per_device(): group_sum = lax.psum(partial_value.astype(jnp.bfloat16), 'cols')  171 us
    psum x1, waiting for transfers between devices, per_device(): summed = lax.psum(group_sum, 'rows').astype(jnp.float32)  138 us
    ppermute x8, waiting for transfers between devices, extended(): after = lax.ppermute(first, axis, down)  32.7 us
    ppermute x8, starting transfers between devices, extended(): after = lax.ppermute(first, axis, down)  19.2 us
    all_to_all x1, blocking collectives, per_device(): lax.all_to_all(filtered, 'cols', split_axis=0, concat_axis=1, tiled=True)  18.4 us
    ppermute x8, starting transfers between devices, extended(): before = lax.ppermute(last, axis, up)  17.4 us
    dot_general x72, matrix products, filter_step(): jnp.einsum('bij,bjc->bic', band_list[position], window, preferred_element...  16.2 us
    all_to_all x1, starting transfers between devices, per_device(): lax.all_to_all(search_vectors, 'cols', split_axis=1, concat_axis=0, tiled...  11.7 us
  transfers between devices with their start and end apart: 19, of which 10 were waited for; matrix products, arithmetic and copies ran while one was open for 3% of the time, Pallas kernels for 0%

commit v1 on v0

v1 whole, which is shorter than its diff:
```python
import functools

import jax
import jax.numpy as jnp
from jax import lax
from jax.experimental import pallas as pl
from jax.experimental.pallas import tpu as pltpu
from jax.sharding import PartitionSpec as P

MESH = pl.DeviceIdType.MESH
BF, F32 = jnp.bfloat16, jnp.float32

TILE = 64
OWN = 16
SIDE = 12
GROUP = 256
WIN = 768
SCALE = 1.0 / 16384

A2A, TIL, IDX, VEC, CUR, OLD = 0, 16, 18, 20, 22, 24
QUART, GATH, PAIR, XRED, ZRED, SPREAD, COUNT = 26, 30, 34, 38, 42, 50, 66


def swap(v):
    return jnp.concatenate([v[:, 64:], v[:, :64]], axis=1)


def pack(block):
    return jnp.concatenate([block[:32], block[32:]], axis=1)


def kernel(
    x_ref, cols_ref, tiles_ref, out_ref, gram_ref,
    xs, xr, tv, th, ab, abh, band, hx, hp, w, y, fp, op, c1, fy, gs, gr, gf, xsnd, xrcv, zs, zr, ro,
    local_sem, ss, rs,
):
    r, c = lax.axis_index("rows"), lax.axis_index("cols")
    yy, zh = lax.rem(c, 4), c // 4
    core, x, zl = lax.rem(r, 2), lax.rem(r // 2, 4), r // 8
    z = zh * 2 + zl

    def remote(src, dst, number, device):
        return pltpu.make_async_remote_copy(
            src_ref=src, dst_ref=dst, send_sem=ss.at[number], recv_sem=rs.at[number],
            device_id=device, device_id_type=MESH,
        )

    own_tiles = pltpu.make_async_copy(tiles_ref, tv, local_sem)
    own_tiles.start()

    barrier = pltpu.get_barrier_semaphore()

    def greet(device):
        pl.semaphore_signal(barrier, inc=1, device_id=device, device_id_type=MESH)

    for i in range(1, 16):
        greet((r, lax.rem(c + i, 16)))
        greet((lax.rem(r + i, 16), c))
    for i in range(1, 4):
        greet((lax.rem(r + 8, 16), lax.rem(zh + i, 4) * 4 + yy))

    for g in range(16):
        xs[g] = pack(x_ref[:, g * 64 : (g + 1) * 64])

    low = lax.broadcasted_iota(jnp.int32, (1, 128), 1) < 64
    for b in range(OWN):
        base = r * OWN + (b // 4) * 4 - 4
        for p in range(4):
            even, odd = cols_ref[b, 2 * p] - base, cols_ref[b, 2 * p + 1] - base
            ab[b, p : p + 1, :] = jnp.where(low, even, odd - 1).astype(F32)
            ab[b, 4 + p : 5 + p, :] = jnp.where(low, odd, even - 1).astype(F32)

    pl.semaphore_wait(barrier, 33)

    a2a = []
    for i in range(1, 16):
        to = lax.rem(c + i, 16)
        copy = remote(xs.at[to], xr.at[c], A2A + i, (r, to))
        copy.start()
        a2a.append(copy)
    xr[c] = xs[c]

    has_low, has_high = r > 0, r < 15
    up, down = jnp.minimum(r + 1, 15), jnp.maximum(r - 1, 0)

    def both_sides(number, to_up, to_down, low_dst, high_dst):
        a = remote(to_up, low_dst, number, (up, c))
        b = remote(to_down, high_dst, number + 1, (down, c))
        pl.when(has_high)(a.start)
        pl.when(has_low)(b.start)
        return a, b

    def arrived(pair):
        pl.when(has_low)(pair[0].wait_recv)
        pl.when(has_high)(pair[1].wait_recv)

    def sent(pair):
        pl.when(has_high)(pair[0].wait_send)
        pl.when(has_low)(pair[1].wait_send)

    idx = both_sides(IDX, ab.at[pl.ds(4, SIDE)], ab.at[pl.ds(0, SIDE)], abh.at[0], abh.at[1])
    til = both_sides(
        TIL, tiles_ref.at[pl.ds(4, SIDE)], tiles_ref.at[pl.ds(0, SIDE)], th.at[0], th.at[1]
    )

    def place(tiles, where, first, count):
        def body(b, carry):
            at = pl.multiple_of((first + b) * TILE, TILE)
            sums = [None] * 6
            for p in range(4):
                src = tiles[b, :, p * 128 : (p + 1) * 128]
                for piece, row in ((src, p), (swap(src), 4 + p)):
                    lanes = where[b, row : row + 1, :]
                    for j in range(6):
                        term = piece * jnp.where(lanes == 2.0 * j, 1.0, 0.0).astype(BF)
                        sums[j] = term if sums[j] is None else sums[j] + term
            for j in range(6):
                band[pl.ds(at, TILE), j * 128 : (j + 1) * 128] = sums[j]
            return carry

        lax.fori_loop(0, count, body, 0)

    own_tiles.wait()
    place(tv, ab, SIDE, OWN)

    def unpack_to(packed, first, targets):
        for b in range(OWN):
            v = packed[b]
            for half in range(2):
                rows = pl.ds((first + b) * TILE + half * 32, 32)
                piece = v[:, half * 64 : (half + 1) * 64]
                for ref in targets:
                    ref[rows, :] = piece.astype(ref.dtype)

    for copy in a2a:
        copy.wait_recv()
    vec = both_sides(VEC, xr, xr, hx.at[0], hx.at[1])
    unpack_to(xr, OWN, (w.at[0], y.at[0]))

    edge = lambda side: has_low if side == 0 else has_high

    def zero(ref, first, count):
        ref[pl.ds(first, count), :] = jnp.zeros((count, ref.shape[1]), ref.dtype)

    arrived(idx)
    arrived(til)
    for side in range(2):
        first = (SIDE + OWN) * side

        @pl.when(edge(side))
        def _(side=side, first=first):
            place(th.at[side], abh.at[side], first, SIDE)

        @pl.when(jnp.logical_not(edge(side)))
        def _(side=side, first=first):
            zero(band, first * TILE, SIDE * TILE)
            for k in range(2):
                zero(w.at[k], side * 2 * OWN * TILE, OWN * TILE)
                zero(y.at[k], side * 2 * OWN * TILE, OWN * TILE)

    arrived(vec)
    for side in range(2):

        @pl.when(edge(side))
        def _(side=side):
            unpack_to(hx.at[side], side * 2 * OWN, (w.at[0], y.at[0]))

    def step(number, first, count):
        now, later = number % 2, (number + 1) % 2

        def body(i, carry):
            for k in range(2):
                g = first + 2 * i + k
                rows = pl.ds(pl.multiple_of(g * GROUP, GROUP), GROUP)
                left = pl.ds(pl.multiple_of((g - 1) * GROUP, GROUP), GROUP)
                window = pl.ds(pl.multiple_of((g - 1) * GROUP, GROUP), WIN)
                product = jnp.dot(band[left, :], w[now, window, :], preferred_element_type=F32)
                if number == 0:
                    new = (product - 0.1 * y[now, rows, :]) * 0.5
                else:
                    new = product - 0.1 * y[now, rows, :] - y[later, rows, :]
                y[later, rows, :] = new
                w[later, rows, :] = new.astype(BF)
            return carry

        lax.fori_loop(0, count // 2, body, 0)

    for n in range(4):
        step(n, 1 + n, 10 - 2 * n)

    def pack_own(src, dst):
        for b in range(OWN):
            dst[b] = pack(src[pl.ds((OWN + b) * TILE, TILE), :]).astype(BF)

    pack_own(w.at[0], fp.at[0])
    cur = both_sides(CUR, fp.at[0], fp.at[0], hp.at[0], hp.at[1])
    pack_own(y.at[1], op)
    old = both_sides(OLD, op, op, hp.at[2], hp.at[3])
    arrived(cur)
    arrived(old)
    for side in range(2):

        @pl.when(edge(side))
        def _(side=side):
            unpack_to(hp.at[side], side * 2 * OWN, (w.at[0], y.at[0]))
            unpack_to(hp.at[2 + side], side * 2 * OWN, (y.at[1],))

    for n in range(4):
        step(4 + n, 1 + n, 10 - 2 * n)

    pack_own(w.at[0], fp.at[1])

    quart = []
    for i in range(1, 4):
        to = lax.rem(zh + i, 4)
        copy = remote(fp.at[1, pl.ds(to * 4, 4)], c1.at[zh], QUART + i, (r, to * 4 + yy))
        copy.start()
        quart.append(copy)
    c1[zh] = fp[1, pl.ds(zh * 4, 4)]
    for copy in quart:
        copy.wait_recv()
    for b in range(4):
        for pair in range(2):
            left, right = c1[2 * pair, b], c1[2 * pair + 1, b]
            for half in range(2):
                lanes = slice(half * 64, (half + 1) * 64)
                fy[yy, pl.ds(b * TILE + half * 32, 32), pair * 128 : (pair + 1) * 128] = (
                    jnp.concatenate([left[:, lanes], right[:, lanes]], axis=1)
                )

    gath = []
    for i in range(1, 4):
        copy = remote(fy.at[yy], fy.at[yy], GATH + i, (r, zh * 4 + lax.rem(yy + i, 4)))
        copy.start()
        gath.append(copy)
    mine_t = fy[yy].astype(F32).T.astype(BF)
    for copy in gath:
        copy.wait_recv()

    pair_dev = (r + 1 - 2 * core, c)
    pairs = []
    for k in range(4):
        gs[k] = jnp.dot(
            mine_t, fy[(1 - core) * 2 + k // 2, :, (k % 2) * 128 : (k % 2 + 1) * 128],
            preferred_element_type=F32,
        ).astype(BF)
        copy = remote(gs.at[k], gr.at[k], PAIR + k, pair_dev)
        copy.start()
        pairs.append(copy)
    for k in range(4):
        gf[k] = jnp.dot(
            mine_t, fy[core * 2 + k // 2, :, (k % 2) * 128 : (k % 2 + 1) * 128],
            preferred_element_type=F32,
        )

    rows = pl.ds(pl.multiple_of(yy * TILE, TILE), TILE)
    for h in range(4):
        for p in range(2):
            lanes = slice(h * 64, (h + 1) * 64)
            out_ref[:, h * 256 + p * 128 : h * 256 + (p + 1) * 128] = jnp.concatenate(
                [fy[2 * p, rows, lanes], fy[2 * p + 1, rows, lanes]], axis=1
            )

    for k in range(4):
        pairs[k].wait_recv()
        total = gf[k] + gr[k].astype(F32)
        gf[k] = total
        xsnd[k] = total.astype(BF)
    xred = []
    for i in range(1, 4):
        to = lax.rem(x + i, 4)
        copy = remote(xsnd.at[to], xrcv.at[i], XRED + i, (zl * 8 + to * 2 + core, c))
        copy.start()
        xred.append(copy)
    total = gf[x]
    for i in range(1, 4):
        xred[i - 1].wait_recv()
        total = total + xrcv[i].astype(F32)
    gf[x] = total
    zs[...] = total.astype(BF)

    zred = []
    for i in range(1, 8):
        to = lax.rem(z + i, 8)
        device = (lax.rem(to, 2) * 8 + x * 2 + core, (to // 2) * 4 + yy)
        copy = remote(zs.at[pl.ds(pl.multiple_of(to * 32, 32), 32)], zr.at[i], ZRED + i, device)
        copy.start()
        zred.append(copy)
    total = gf[x, pl.ds(pl.multiple_of(z * 32, 32), 32), :]
    for i in range(1, 8):
        zred[i - 1].wait_recv()
        total = total + zr[i].astype(F32)
    ro[r] = total * SCALE

    spread = []
    for i in range(1, 16):
        copy = remote(ro.at[r], ro.at[r], SPREAD + i, (lax.rem(r + i, 16), c))
        copy.start()
        spread.append(copy)

    sent(idx)
    sent(til)
    sent(vec)
    sent(cur)
    sent(old)
    for copy in a2a + quart + gath + pairs + xred + zred:
        copy.wait_send()
    for copy in spread:
        copy.wait_recv()
    for l in range(2):
        for h in range(4):
            for p in range(2):
                lanes = slice((h % 2) * 64, (h % 2 + 1) * 64)
                at = [l * 8 + (k * 2 + h // 2) * 2 + p for k in range(2)]
                gram_ref[l * 32 : (l + 1) * 32, h * 256 + p * 128 : h * 256 + (p + 1) * 128] = (
                    jnp.concatenate([ro[at[0]][:, lanes], ro[at[1]][:, lanes]], axis=1)
                )
    for copy in spread:
        copy.wait_send()


def per_device(search_vectors, tile_values, block_columns):
    ext = 3 * OWN * TILE
    return pl.pallas_call(
        kernel,
        out_shape=(
            jax.ShapeDtypeStruct((64, 1024), BF),
            jax.ShapeDtypeStruct((64, 1024), F32),
        ),
        in_specs=[
            pl.BlockSpec(memory_space=pltpu.VMEM),
            pl.BlockSpec(memory_space=pltpu.SMEM),
            pl.BlockSpec(memory_space=pl.ANY),
        ],
        out_specs=(pl.BlockSpec(memory_space=pltpu.VMEM), pl.BlockSpec(memory_space=pltpu.VMEM)),
        scratch_shapes=[
            pltpu.VMEM((16, 32, 128), BF),
            pltpu.VMEM((16, 32, 128), BF),
            pltpu.VMEM((OWN, TILE, 512), BF),
            pltpu.VMEM((2, SIDE, TILE, 512), BF),
            pltpu.VMEM((OWN, 8, 128), F32),
            pltpu.VMEM((2, SIDE, 8, 128), F32),
            pltpu.VMEM(((2 * SIDE + OWN) * TILE, WIN), BF),
            pltpu.VMEM((2, 16, 32, 128), BF),
            pltpu.VMEM((4, 16, 32, 128), BF),
            pltpu.VMEM((2, ext, 64), BF),
            pltpu.VMEM((2, ext, 64), F32),
            pltpu.VMEM((2, 16, 32, 128), BF),
            pltpu.VMEM((16, 32, 128), BF),
            pltpu.VMEM((4, 4, 32, 128), BF),
            pltpu.VMEM((4, 256, 256), BF),
            pltpu.VMEM((4, 256, 128), BF),
            pltpu.VMEM((4, 256, 128), BF),
            pltpu.VMEM((4, 256, 128), F32),
            pltpu.VMEM((4, 256, 128), BF),
            pltpu.VMEM((4, 256, 128), BF),
            pltpu.VMEM((256, 128), BF),
            pltpu.VMEM((8, 32, 128), BF),
            pltpu.VMEM((16, 32, 128), F32),
            pltpu.SemaphoreType.DMA,
            pltpu.SemaphoreType.DMA((COUNT,)),
            pltpu.SemaphoreType.DMA((COUNT,)),
        ],
        compiler_params=pltpu.CompilerParams(
            collective_id=0, has_side_effects=True, vmem_limit_bytes=48 * 1024 * 1024
        ),
        name="filter_and_gram",
    )(search_vectors, block_columns, tile_values)


def solution(mesh):
    return jax.shard_map(
        per_device,
        mesh=mesh,
        in_specs=(P(("rows", "cols"), None), P("rows", None, None), P("rows", None)),
        out_specs=(P(("rows", "cols"), None), P("cols", None)),
        check_vma=False,
    )
```

time: 464 us -> 80.3 us (0.17)
  waiting for transfers between devices: 342 us -> 0 us
  Pallas kernels: 0 us -> 75.3 us
  starting transfers between devices: 48.4 us -> 0 us
  matrix products: 24.5 us -> 0 us
  blocking collectives: 18.4 us -> 0 us
  between operations: 15 us -> 0.64 us
  other arithmetic: 8.8 us -> 0 us
    psum x2 -> x0, waiting for transfers between devices: 309 us -> none  [the longest x1 171 us: per_device(): group_sum = lax.psum(partial_value.astype(jnp.bfloat16), 'cols')]
    pallas_call x0 -> x1, Pallas kernels: none -> 75.3 us  [per_device(): pl.pallas_call(kernel, out_shape=(jax.ShapeDtypeStruct((64, 1024), BF), j...]
    ppermute x16 -> x0, starting transfers between devices: 36.6 us -> none  [the longest x8 19.2 us: extended(): after = lax.ppermute(first, axis, down)]
    ppermute x16 -> x0, waiting for transfers between devices: 32.7 us -> none  [the longest x8 32.7 us: extended(): after = lax.ppermute(first, axis, down)]
    dot_general x82 -> x0, matrix products: 24.5 us -> none  [the longest x72 16.2 us: filter_step(): jnp.einsum('bij,bjc->bic', band_list[position], window, preferred_element...]
    all_to_all x1 -> x0, blocking collectives: 18.4 us -> none  [per_device(): lax.all_to_all(filtered, 'cols', split_axis=0, concat_axis=1, tiled=True)]
    all_to_all x1 -> x0, starting transfers between devices: 11.7 us -> none  [per_device(): lax.all_to_all(search_vectors, 'cols', split_axis=1, concat_axis=0, tiled...]
  transfers between devices with their start and end apart: 19 -> 0, of which waited for: 10 -> 0; matrix products, arithmetic and copies ran while one was open for 3% -> 0% of each run, Pallas kernels for 0% -> 0%
where the time goes in v1:
time: 80.3 us; the launch traced here: 80.1 us
  Pallas kernels  75.3 us (94%)
  local copies, waits for them, and re-layouts  4.25 us (5%)
    pallas_call x1, Pallas kernels, per_device(): pl.pallas_call(kernel, out_shape=(jax.ShapeDtypeStruct((64, 1024), BF), j...  75.3 us
    unnamed x7, local copies, waits for them, and re-layouts  4.25 us

profile of v1, /device:TPU:1, one launch (start us, length us, event | category | flops | bytes accessed | tf_op | source)
XLA Modules:
  0.0 80.1 jit_solution(15056630549184072930)
XLA Ops:
  0.6 0.8 copy.5.cols_ref
  1.4 0.0 copy-start
  1.4 1.2 %copy-done = bf16[16,64,512]{2,1,0:T(8,128)(2,1)S(1)} copy-done((bf16[16,64,512]{2,1,0:T(8,128)(2,1)S(1)}, bf16[16,64,512]{2,1,0:T(8,128)(2,1)}, u32[]{:S(2)}) %copy-start) | copy-done | bytes 1048600
  2.6 0.0 copy-start.1
  2.6 0.9 %copy-done.1 = bf16[64,1024]{1,0:T(8,128)(2,1)S(1)} copy-done((bf16[64,1024]{1,0:T(8,128)(2,1)S(1)}, bf16[64,1024]{1,0:T(8,128)(2,1)}, u32[]{:S(2)}) %copy-start.1) | copy-done | bytes 131096
  3.5 75.3 %filter_and_gram.1 = (bf16[64,1024]{1,0:T(8,128)(2,1)S(1)}, f32[64,1024]{1,0:T(8,128)S(1)}) custom-call(bf16[64,1024]{1,0:T(8,128)(2,1)S(1)} %copy-done.1, s32[16,8]{1,0:T(8,128)S(1)} %copy.5.cols_ref, bf16[16,64,512]{2,1,0:T(8,128)(2,1)S(1)} %copy-done), custom_call_target="tpu_custom_call" | custom-call | tf_op jit(solution)/shard_map/filter_and_gram/pallas_call | solution.py:324
  78.8 0.7 copy.8
  79.4 0.7 copy.9
Async XLA Ops:
  1.4 1.2 %copy-start = (bf16[16,64,512]{2,1,0:T(8,128)(2,1)S(1)}, bf16[16,64,512]{2,1,0:T(8,128)(2,1)}, u32[]{:S(2)}) copy-start(bf16[16,64,512]{2,1,0:T(8,128)(2,1)} %tiles_ref.1) | copy-start | bytes 3145732
  2.6 0.9 %copy-start.1 = (bf16[64,1024]{1,0:T(8,128)(2,1)S(1)}, bf16[64,1024]{1,0:T(8,128)(2,1)}, u32[]{:S(2)}) copy-start(bf16[64,1024]{1,0:T(8,128)(2,1)} %x_ref.1) | copy-start | bytes 393220

commit v2 on v0

v2 whole, which is shorter than its diff:
```python
import jax
import jax.numpy as jnp
from jax import lax
from jax.experimental import pallas as pl
from jax.experimental.pallas import tpu as pltpu
from jax.sharding import PartitionSpec as P

MESH = pl.DeviceIdType.MESH
BF, F32 = jnp.bfloat16, jnp.float32

TILE = 64
OWN = 16
GROUP = 256
WIN = 768
SCALE = 1.0 / 16384

A2A, TIL, IDX, VEC, EARLY, OLD, LATE = 0, 16, 22, 24, 26, 28, 30
QUART, GATH, PAIR, XRED, ZRED, SPREAD, COUNT = 32, 36, 52, 56, 60, 68, 84


def swap(v):
    return jnp.concatenate([v[:, 64:], v[:, :64]], axis=1)


def pack(block):
    return jnp.concatenate([block[:32], block[32:]], axis=1)


def kernel(
    x_hbm, cols_hbm, tiles_hbm, out_ref, gram_ref,
    x_ref, cols_ref, xs, xr, tv, th, idxv, idxh, idxs, slab, band, hx, hp, ho, w, y,
    fp, op, fq, pc, fy, gs, gr, gf, xsnd, xrcv, zs, zr, ro, local_sem, ss, rs,
):
    r, c = lax.axis_index("rows"), lax.axis_index("cols")
    yy, zh = lax.rem(c, 4), c // 4
    core, x, zl = lax.rem(r, 2), lax.rem(r // 2, 4), r // 8
    z = zh * 2 + zl

    def remote(src, dst, number, device):
        return pltpu.make_async_remote_copy(
            src_ref=src, dst_ref=dst, send_sem=ss.at[number], recv_sem=rs.at[number],
            device_id=device, device_id_type=MESH,
        )

    own_x = pltpu.make_async_copy(x_hbm, x_ref, local_sem.at[0])
    own_cols = pltpu.make_async_copy(cols_hbm, cols_ref, local_sem.at[1])
    own_tiles = pltpu.make_async_copy(tiles_hbm, tv, local_sem.at[2])

    barrier = pltpu.get_barrier_semaphore()

    def greet(device):
        pl.semaphore_signal(barrier, inc=1, device_id=device, device_id_type=MESH)

    for i in (8, 7, 9, 6, 10, 5, 11, 4, 12, 3, 13, 2, 14, 1, 15):
        greet((r, lax.rem(c + i, 16)))
        greet((lax.rem(r + i, 16), c))
    for i in range(1, 4):
        greet((lax.rem(r + 8, 16), lax.rem(zh + i, 4) * 4 + yy))
    own_x.start()
    own_cols.start()
    own_tiles.start()

    has_low, has_high = r > 0, r < 15
    edges = (has_low, has_high)
    up, down = jnp.minimum(r + 1, 15), jnp.maximum(r - 1, 0)

    def zero(ref, first, count):
        ref[pl.ds(first, count), :] = jnp.zeros((count, ref.shape[1]), ref.dtype)

    for side in range(2):

        @pl.when(jnp.logical_not(edges[side]))
        def _(side=side):
            zero(band, 7 * side * GROUP, 3 * GROUP)
            for k in range(2):
                zero(w.at[k], side * 8 * GROUP, 4 * GROUP)
                zero(y.at[k], side * 8 * GROUP, 4 * GROUP)

    for u in range(4):
        slab[u, 8] = jnp.zeros((TILE, 128), BF)

    own_x.wait()
    for g in range(16):
        xs[g] = pack(x_ref[:, g * 64 : (g + 1) * 64])

    own_cols.wait()
    slot = lax.broadcasted_iota(jnp.int32, (16, OWN), 0)
    first_col = r * OWN + (lax.broadcasted_iota(jnp.int32, (8, OWN), 1) // 4) * 4 - 4
    places = cols_ref[...] - first_col
    slabs = jnp.full((16, OWN), 8, jnp.int32)
    for k in range(8):
        which = jnp.where(lax.rem(slot, 2) == 0, k, k + 1 - 2 * (k % 2))
        slabs = jnp.where(slot == places[k : k + 1, :], which, slabs)
    idxv[...] = jnp.zeros_like(idxv)
    idxv[:, :OWN] = slabs

    pl.semaphore_wait(barrier, 33)

    a2a = []
    for i in (8, 7, 9, 6, 10, 5, 11, 4, 12, 3, 13, 2, 14, 1, 15):
        to = lax.rem(c + i, 16)
        copy = remote(xs.at[to], xr.at[c], A2A + i, (r, to))
        copy.start()
        a2a.append(copy)

    def both_sides(number, to_up, to_down, low_dst, high_dst):
        a = remote(to_up, low_dst, number, (up, c))
        b = remote(to_down, high_dst, number + 1, (down, c))
        pl.when(has_high)(a.start)
        pl.when(has_low)(b.start)
        return a, b

    def arrived(pair):
        pl.when(has_low)(pair[0].wait_recv)
        pl.when(has_high)(pair[1].wait_recv)

    def sent(pair):
        pl.when(has_high)(pair[0].wait_send)
        pl.when(has_low)(pair[1].wait_send)

    idx = both_sides(IDX, idxv, idxv, idxh.at[0], idxh.at[1])
    til = [
        both_sides(
            TIL + 2 * n, tiles_hbm.at[pl.ds(4 * (3 - n), 4)], tiles_hbm.at[pl.ds(4 * n, 4)],
            th.at[0, n], th.at[1, n],
        )
        for n in range(3)
    ]
    xr[c] = xs[c]

    low_lanes = lax.broadcasted_iota(jnp.int32, (TILE, 128), 1) < 64

    def place(tiles, source, first, at):
        for u in range(4):
            for p in range(4):
                piece = tiles[u, :, p * 128 : (p + 1) * 128]
                slab[u, 2 * p] = piece
                slab[u, 2 * p + 1] = swap(piece)
            for j in range(6):
                left = slab[u, idxs[source, 2 * j, first + u]]
                right = slab[u, idxs[source, 2 * j + 1, first + u]]
                band[pl.ds(at + u * TILE, TILE), j * 128 : (j + 1) * 128] = jnp.where(
                    low_lanes, left, right
                )

    def to_smem(src, number):
        copy = pltpu.make_async_copy(src, idxs.at[number], local_sem.at[3])
        copy.start()
        copy.wait()

    to_smem(idxv, 2)
    own_tiles.wait()

    def place_own(i, carry):
        at = pl.multiple_of((3 + i) * GROUP, GROUP)
        place(tv.at[pl.ds(4 * i, 4)], 2, 4 * i, at)
        return carry

    lax.fori_loop(0, 4, place_own, 0)

    def unpack(v, block, targets):
        for half in range(2):
            rows = pl.ds(block * TILE + half * 32, 32)
            piece = v[:, half * 64 : (half + 1) * 64]
            for ref in targets:
                ref[rows, :] = piece.astype(ref.dtype)

    def one(n, g):
        now, later = n % 2, (n + 1) % 2
        at = g * GROUP if isinstance(g, int) else pl.multiple_of(g * GROUP, GROUP)
        back = (g - 1) * GROUP if isinstance(g, int) else pl.multiple_of((g - 1) * GROUP, GROUP)
        rows = pl.ds(at, GROUP)
        product = jnp.dot(
            band[pl.ds(back, GROUP), :], w[now, pl.ds(back, WIN), :], preferred_element_type=F32
        )
        if n == 0:
            new = (product - 0.1 * y[now, rows, :]) * 0.5
        else:
            new = product - 0.1 * y[now, rows, :] - y[later, rows, :]
        rounded = new.astype(BF)
        if n < 7:
            y[later, rows, :] = new
            w[later, rows, :] = rounded
        return rounded

    for copy in a2a:
        copy.wait_recv()
    vec = both_sides(VEC, xr, xr, hx.at[0], hx.at[1])
    for b in range(OWN):
        unpack(xr[b], OWN + b, (w.at[0], y.at[0]))
    for g in (5, 6):
        one(0, g)

    arrived(vec)
    for side in range(2):

        @pl.when(edges[side])
        def _(side=side):
            for b in range(OWN):
                unpack(hx[side, b], side * 2 * OWN + b, (w.at[0], y.at[0]))

    for n, g in ((0, 4), (0, 7), (1, 5), (1, 6)):
        one(n, g)

    arrived(idx)
    for side in range(2):

        @pl.when(edges[side])
        def _(side=side):
            to_smem(idxh.at[side], side)

    def halo_tiles(n):
        arrived(til[n])
        for side in range(2):

            @pl.when(edges[side])
            def _(side=side):
                place(
                    th.at[side, n], side, 4 * (3 - n) if side == 0 else 4 * n,
                    (2 - n if side == 0 else 7 + n) * GROUP,
                )

    halo_tiles(0)
    for n, g in ((0, 3), (0, 8), (1, 4), (1, 7), (2, 5), (2, 6)):
        one(n, g)
    halo_tiles(1)
    for n, g in ((0, 2), (0, 9), (1, 3), (1, 8), (2, 4), (2, 7)):
        one(n, g)

    for b in range(8):
        op[b] = pack(y[1, pl.ds((20 + b) * TILE, TILE), :]).astype(BF)
    old = both_sides(OLD, op, op, ho.at[0], ho.at[1])

    def pack_group(rounded, dst, first):
        for b in range(4):
            dst[first + b] = pack(rounded[b * TILE : (b + 1) * TILE])

    for slot, g in ((0, 5), (4, 6)):
        pack_group(one(3, g), fp, slot)
    early = both_sides(
        EARLY, fp.at[pl.ds(0, 8)], fp.at[pl.ds(0, 8)], hp.at[0, pl.ds(0, 8)], hp.at[1, pl.ds(0, 8)]
    )
    halo_tiles(2)
    for n, g in ((0, 1), (0, 10), (1, 2), (1, 9), (2, 3), (2, 8)):
        one(n, g)
    for slot, g in ((8, 4), (12, 7)):
        pack_group(one(3, g), fp, slot)
    late = both_sides(
        LATE, fp.at[pl.ds(8, 8)], fp.at[pl.ds(8, 8)], hp.at[0, pl.ds(8, 8)], hp.at[1, pl.ds(8, 8)]
    )
    for g in (5, 6):
        one(4, g)

    arrived(old)
    arrived(early)
    for side in range(2):

        @pl.when(edges[side])
        def _(side=side):
            for b in range(8):
                unpack(hp[side, b], side * 2 * OWN + 4 + b, (w.at[0], y.at[0]))
                unpack(ho[side, b], side * 2 * OWN + 4 + b, (y.at[1],))

    arrived(late)
    for side in range(2):

        @pl.when(edges[side])
        def _(side=side):
            for b in range(8):
                block = b if b < 4 else b + 8
                unpack(hp[side, 8 + b], side * 2 * OWN + block, (w.at[0], y.at[0]))

    for g in (3, 4, 7, 8, 2, 9, 1, 10):
        one(4, g)
    for g in (5, 6, 4, 7, 3, 8, 2, 9):
        one(5, g)
    for g in (5, 6, 4, 7, 3, 8):
        one(6, g)

    quart, gath = [], []
    for i in (2, 1, 3, 0):
        to = lax.rem(zh + i, 4)
        rounded = one(7, 4 + to)
        if i:
            pack_group(rounded, fq.at[to], 0)
            copy = remote(fq.at[to], pc.at[yy, zh], QUART + i, (r, to * 4 + yy))
            copy.start()
            quart.append((i, copy))
        else:
            pack_group(rounded, pc.at[yy, zh], 0)

    def to_y(i):
        piece = pc.at[yy, lax.rem(zh - i + 4, 4)]
        for j in (2, 1, 3):
            device = (r, zh * 4 + lax.rem(yy + j, 4))
            copy = remote(piece, piece, GATH + 4 * i + j, device)
            copy.start()
            gath.append(copy)

    to_y(0)
    for i, copy in (quart[1], quart[2], quart[0]):
        copy.wait_recv()
        to_y(i)

    def assemble(who):
        for half in range(2):
            for b in range(4):
                left, right = pc[who, 2 * half, b], pc[who, 2 * half + 1, b]
                for part in range(2):
                    lanes = slice(part * 64, (part + 1) * 64)
                    fy[2 * who + half, pl.ds(b * TILE + part * 32, 32), :] = jnp.concatenate(
                        [left[:, lanes], right[:, lanes]], axis=1
                    )

    assemble(yy)
    mine = jnp.concatenate(
        [fy[2 * yy + half].astype(F32).T.astype(BF) for half in range(2)], axis=0
    )
    for copy in gath:
        copy.wait_recv()
    for j in range(1, 4):
        assemble(lax.rem(yy + j, 4))

    pair_dev = (r + 1 - 2 * core, c)
    order = (2, 1, 3, 0)
    pairs = {}
    for i in order:
        to = lax.rem(x + i, 4)
        gs[i] = jnp.dot(mine, fy[(1 - core) * 4 + to], preferred_element_type=F32).astype(BF)
        pairs[i] = remote(gs.at[i], gr.at[i], PAIR + i, pair_dev)
        pairs[i].start()
    for i in order:
        gf[i] = jnp.dot(mine, fy[core * 4 + lax.rem(x + i, 4)], preferred_element_type=F32)

    xred = []
    for i in order:
        pairs[i].wait_recv()
        total = gf[i] + gr[i].astype(F32)
        if i:
            to = lax.rem(x + i, 4)
            xsnd[i] = total.astype(BF)
            copy = remote(xsnd.at[i], xrcv.at[i], XRED + i, (zl * 8 + to * 2 + core, c))
            copy.start()
            xred.append((i, copy))

    rows = pl.ds(pl.multiple_of(yy * TILE, TILE), TILE)
    for h in range(4):
        for p in range(2):
            lanes = slice((h % 2) * 64, (h % 2 + 1) * 64)
            out_ref[:, h * 256 + p * 128 : h * 256 + (p + 1) * 128] = jnp.concatenate(
                [fy[4 * p + h // 2, rows, lanes], fy[4 * p + 2 + h // 2, rows, lanes]], axis=1
            )

    for i, copy in xred:
        copy.wait_recv()
        total = total + xrcv[i].astype(F32)
    gf[0] = total
    zs[...] = total.astype(BF)

    zred = []
    for i in (4, 3, 5, 2, 6, 1, 7):
        to = lax.rem(z + i, 8)
        device = (lax.rem(to, 2) * 8 + x * 2 + core, (to // 2) * 4 + yy)
        copy = remote(zs.at[pl.ds(pl.multiple_of(to * 32, 32), 32)], zr.at[i], ZRED + i, device)
        copy.start()
        zred.append((i, copy))
    total = gf[0, pl.ds(pl.multiple_of(z * 32, 32), 32), :]
    for i, copy in zred:
        copy.wait_recv()
        total = total + zr[i].astype(F32)
    ro[r] = (total * SCALE).astype(BF)

    spread = []
    for i in (8, 7, 9, 6, 10, 5, 11, 4, 12, 3, 13, 2, 14, 1, 15):
        copy = remote(ro.at[r], ro.at[r], SPREAD + i, (lax.rem(r + i, 16), c))
        copy.start()
        spread.append(copy)

    for pair in (idx, *til, vec, old, early, late):
        sent(pair)
    for copy in a2a + gath:
        copy.wait_send()
    for i, copy in quart + list(pairs.items()) + xred + zred:
        copy.wait_send()
    for copy in spread:
        copy.wait_recv()
    for l in range(2):
        for h in range(4):
            for p in range(2):
                lanes = slice((h % 2) * 64, (h % 2 + 1) * 64)
                at = [l * 8 + (k * 2 + h // 2) * 2 + p for k in range(2)]
                gram_ref[l * 32 : (l + 1) * 32, h * 256 + p * 128 : h * 256 + (p + 1) * 128] = (
                    jnp.concatenate([ro[at[0]][:, lanes], ro[at[1]][:, lanes]], axis=1).astype(F32)
                )
    for copy in spread:
        copy.wait_send()


def per_device(search_vectors, tile_values, block_columns):
    ext = 12 * GROUP
    return pl.pallas_call(
        kernel,
        out_shape=(
            jax.ShapeDtypeStruct((64, 1024), BF),
            jax.ShapeDtypeStruct((64, 1024), F32),
        ),
        in_specs=[pl.BlockSpec(memory_space=pl.ANY)] * 3,
        out_specs=(pl.BlockSpec(memory_space=pltpu.VMEM), pl.BlockSpec(memory_space=pltpu.VMEM)),
        scratch_shapes=[
            pltpu.VMEM((64, 1024), BF),
            pltpu.VMEM((8, OWN), jnp.int32),
            pltpu.VMEM((16, 32, 128), BF),
            pltpu.VMEM((16, 32, 128), BF),
            pltpu.VMEM((OWN, TILE, 512), BF),
            pltpu.VMEM((2, 3, 4, TILE, 512), BF),
            pltpu.VMEM((16, 128), jnp.int32),
            pltpu.VMEM((2, 16, 128), jnp.int32),
            pltpu.SMEM((3, 16, 128), jnp.int32),
            pltpu.VMEM((4, 9, TILE, 128), BF),
            pltpu.VMEM((10 * GROUP, WIN), BF),
            pltpu.VMEM((2, 16, 32, 128), BF),
            pltpu.VMEM((2, 16, 32, 128), BF),
            pltpu.VMEM((2, 8, 32, 128), BF),
            pltpu.VMEM((2, ext, 64), BF),
            pltpu.VMEM((2, ext, 64), F32),
            pltpu.VMEM((16, 32, 128), BF),
            pltpu.VMEM((8, 32, 128), BF),
            pltpu.VMEM((4, 4, 32, 128), BF),
            pltpu.VMEM((4, 4, 4, 32, 128), BF),
            pltpu.VMEM((8, 256, 128), BF),
            pltpu.VMEM((4, 256, 128), BF),
            pltpu.VMEM((4, 256, 128), BF),
            pltpu.VMEM((4, 256, 128), F32),
            pltpu.VMEM((4, 256, 128), BF),
            pltpu.VMEM((4, 256, 128), BF),
            pltpu.VMEM((256, 128), BF),
            pltpu.VMEM((8, 32, 128), BF),
            pltpu.VMEM((16, 32, 128), BF),
            pltpu.SemaphoreType.DMA((4,)),
            pltpu.SemaphoreType.DMA((COUNT,)),
            pltpu.SemaphoreType.DMA((COUNT,)),
        ],
        compiler_params=pltpu.CompilerParams(
            collective_id=0, has_side_effects=True, vmem_limit_bytes=48 * 1024 * 1024
        ),
        name="filter_and_gram",
    )(*(pltpu.with_memory_space_constraint(v, pltpu.HBM) for v in (search_vectors, block_columns.T, tile_values)))


def solution(mesh):
    return jax.shard_map(
        per_device,
        mesh=mesh,
        in_specs=(P(("rows", "cols"), None), P("rows", None, None), P("rows", None)),
        out_specs=(P(("rows", "cols"), None), P("cols", None)),
        check_vma=False,
    )
```

time: 464 us -> 68.4 us (0.15)
  waiting for transfers between devices: 342 us -> 0 us
  Pallas kernels: 0 us -> 66.3 us
  starting transfers between devices: 48.4 us -> 0 us
  matrix products: 24.5 us -> 0 us
  blocking collectives: 18.4 us -> 0 us
  between operations: 15 us -> 0.64 us
  other arithmetic: 8.8 us -> 0 us
  local copies, waits for them, and re-layouts: 6.7 us -> 1.36 us
    psum x2 -> x0, waiting for transfers between devices: 309 us -> none  [the longest x1 171 us: per_device(): group_sum = lax.psum(partial_value.astype(jnp.bfloat16), 'cols')]
    pallas_call x0 -> x1, Pallas kernels: none -> 66.3 us  [per_device(): pl.pallas_call(kernel, out_shape=(jax.ShapeDtypeStruct((64, 1024), BF), j...]
    ppermute x16 -> x0, starting transfers between devices: 36.6 us -> none  [the longest x8 19.2 us: extended(): after = lax.ppermute(first, axis, down)]
    ppermute x16 -> x0, waiting for transfers between devices: 32.7 us -> none  [the longest x8 32.7 us: extended(): after = lax.ppermute(first, axis, down)]
    dot_general x82 -> x0, matrix products: 24.5 us -> none  [the longest x72 16.2 us: filter_step(): jnp.einsum('bij,bjc->bic', band_list[position], window, preferred_element...]
    all_to_all x1 -> x0, blocking collectives: 18.4 us -> none  [per_device(): lax.all_to_all(filtered, 'cols', split_axis=0, concat_axis=1, tiled=True)]
    all_to_all x1 -> x0, starting transfers between devices: 11.7 us -> none  [per_device(): lax.all_to_all(search_vectors, 'cols', split_axis=1, concat_axis=0, tiled...]
  transfers between devices with their start and end apart: 19 -> 0, of which waited for: 10 -> 0; matrix products, arithmetic and copies ran while one was open for 3% -> 0% of each run, Pallas kernels for 0% -> 0%
where the time goes in v2:
time: 68.4 us; the launch traced here: 68.3 us
  Pallas kernels  66.3 us (97%)
  local copies, waits for them, and re-layouts  1.36 us (2%)
    pallas_call x1, Pallas kernels, per_device(): pl.pallas_call(kernel, out_shape=(jax.ShapeDtypeStruct((64, 1024), BF), j...  66.3 us

profile of v2, /device:TPU:1, one launch (start us, length us, event | category | flops | bytes accessed | tf_op | source)
XLA Modules:
  0.0 68.3 jit_solution(7955645329478872175)
XLA Ops:
  0.6 66.3 %filter_and_gram.1 = (bf16[64,1024]{1,0:T(8,128)(2,1)S(1)}, f32[64,1024]{1,0:T(8,128)S(1)}) custom-call(bf16[64,1024]{1,0:T(8,128)(2,1)} %x_hbm.1, s32[8,16]{1,0:T(8,128)} %bitcast.1, bf16[16,64,512]{2,1,0:T(8,128)(2,1)} %tiles_hbm.1), custom_call_target="tpu_custom_call" | custom-call | tf_op jit(solution)/shard_map/filter_and_gram/pallas_call | solution.py:401
  66.9 0.7 copy.7
  67.6 0.7 %copy.8 = f32[64,1024]{1,0:T(8,128)} copy(f32[64,1024]{1,0:T(8,128)S(1)} %get-tuple-element.5) | data formatting | bytes 524288

commit v3 on v2

--- a/solution.py
+++ b/solution.py
@@ -56,6 +56,10 @@
         greet((lax.rem(r + i, 16), c))
     for i in range(1, 4):
         greet((lax.rem(r + 8, 16), lax.rem(zh + i, 4) * 4 + yy))
+    at_7, at_8 = r == 7, r == 8
+    middle = jnp.logical_or(at_7, at_8)
+    turned = jnp.where(at_7, lax.rem(zh + 3, 4), lax.rem(zh + 1, 4)) * 4 + yy
+    pl.when(middle)(lambda: greet((15 - r, turned)))
     own_x.start()
     own_cols.start()
     own_tiles.start()
@@ -72,9 +76,7 @@
         @pl.when(jnp.logical_not(edges[side]))
         def _(side=side):
             zero(band, 7 * side * GROUP, 3 * GROUP)
-            for k in range(2):
-                zero(w.at[k], side * 8 * GROUP, 4 * GROUP)
-                zero(y.at[k], side * 8 * GROUP, 4 * GROUP)
+            zero(w.at[0], side * 8 * GROUP, 4 * GROUP)
 
     for u in range(4):
         slab[u, 8] = jnp.zeros((TILE, 128), BF)
@@ -94,7 +96,8 @@
     idxv[...] = jnp.zeros_like(idxv)
     idxv[:, :OWN] = slabs
 
-    pl.semaphore_wait(barrier, 33)
+    pl.when(middle)(lambda: pl.semaphore_wait(barrier, 34))
+    pl.when(jnp.logical_not(middle))(lambda: pl.semaphore_wait(barrier, 33))
 
     a2a = []
     for i in (8, 7, 9, 6, 10, 5, 11, 4, 12, 3, 13, 2, 14, 1, 15):
@@ -103,9 +106,9 @@
         copy.start()
         a2a.append(copy)
 
-    def both_sides(number, to_up, to_down, low_dst, high_dst):
-        a = remote(to_up, low_dst, number, (up, c))
-        b = remote(to_down, high_dst, number + 1, (down, c))
+    def both_sides(number, to_up, to_down, low_dst, high_dst, col_up=c, col_down=c):
+        a = remote(to_up, low_dst, number, (up, col_up))
+        b = remote(to_down, high_dst, number + 1, (down, col_down))
         pl.when(has_high)(a.start)
         pl.when(has_low)(b.start)
         return a, b
@@ -123,6 +126,7 @@
         both_sides(
             TIL + 2 * n, tiles_hbm.at[pl.ds(4 * (3 - n), 4)], tiles_hbm.at[pl.ds(4 * n, 4)],
             th.at[0, n], th.at[1, n],
+            *((jnp.where(at_7, turned, c), jnp.where(at_8, turned, c)) if n == 1 else (c, c)),
         )
         for n in range(3)
     ]
@@ -158,12 +162,10 @@
 
     lax.fori_loop(0, 4, place_own, 0)
 
-    def unpack(v, block, targets):
+    def unpack(v, block, ref):
         for half in range(2):
             rows = pl.ds(block * TILE + half * 32, 32)
-            piece = v[:, half * 64 : (half + 1) * 64]
-            for ref in targets:
-                ref[rows, :] = piece.astype(ref.dtype)
+            ref[rows, :] = v[:, half * 64 : (half + 1) * 64].astype(ref.dtype)
 
     def one(n, g):
         now, later = n % 2, (n + 1) % 2
@@ -173,10 +175,13 @@
         product = jnp.dot(
             band[pl.ds(back, GROUP), :], w[now, pl.ds(back, WIN), :], preferred_element_type=F32
         )
+        outer = n in (4, 5) and not 4 <= g <= 7
+        current = w[now, rows, :].astype(F32) if n == 0 or (n == 4 and outer) else y[now, rows, :]
         if n == 0:
-            new = (product - 0.1 * y[now, rows, :]) * 0.5
+            new = (product - 0.1 * current) * 0.5
         else:
-            new = product - 0.1 * y[now, rows, :] - y[later, rows, :]
+            before = w if n == 1 or (n == 5 and outer) else y
+            new = product - 0.1 * current - before[later, rows, :].astype(F32)
         rounded = new.astype(BF)
         if n < 7:
             y[later, rows, :] = new
@@ -187,20 +192,9 @@
         copy.wait_recv()
     vec = both_sides(VEC, xr, xr, hx.at[0], hx.at[1])
     for b in range(OWN):
-        unpack(xr[b], OWN + b, (w.at[0], y.at[0]))
+        unpack(xr[b], OWN + b, w.at[0])
     for g in (5, 6):
         one(0, g)
-
-    arrived(vec)
-    for side in range(2):
-
-        @pl.when(edges[side])
-        def _(side=side):
-            for b in range(OWN):
-                unpack(hx[side, b], side * 2 * OWN + b, (w.at[0], y.at[0]))
-
-    for n, g in ((0, 4), (0, 7), (1, 5), (1, 6)):
-        one(n, g)
 
     arrived(idx)
     for side in range(2):
@@ -221,11 +215,22 @@
                 )
 
     halo_tiles(0)
-    for n, g in ((0, 3), (0, 8), (1, 4), (1, 7), (2, 5), (2, 6)):
-        one(n, g)
     halo_tiles(1)
-    for n, g in ((0, 2), (0, 9), (1, 3), (1, 8), (2, 4), (2, 7)):
-        one(n, g)
+
+    arrived(vec)
+    for side in range(2):
+
+        @pl.when(edges[side])
+        def _(side=side):
+            for b in range(OWN):
+                unpack(hx[side, b], side * 2 * OWN + b, w.at[0])
+
+    for g in (4, 7, 3, 8, 2, 9):
+        one(0, g)
+    for g in (5, 6, 4, 7, 3, 8):
+        one(1, g)
+    for g in (5, 6, 4, 7):
+        one(2, g)
 
     for b in range(8):
         op[b] = pack(y[1, pl.ds((20 + b) * TILE, TILE), :]).astype(BF)
@@ -258,8 +263,8 @@
         @pl.when(edges[side])
         def _(side=side):
             for b in range(8):
-                unpack(hp[side, b], side * 2 * OWN + 4 + b, (w.at[0], y.at[0]))
-                unpack(ho[side, b], side * 2 * OWN + 4 + b, (y.at[1],))
+                unpack(hp[side, b], side * 2 * OWN + 4 + b, w.at[0])
+                unpack(ho[side, b], side * 2 * OWN + 4 + b, y.at[1])
 
     arrived(late)
     for side in range(2):
@@ -268,7 +273,7 @@
         def _(side=side):
             for b in range(8):
                 block = b if b < 4 else b + 8
-                unpack(hp[side, 8 + b], side * 2 * OWN + block, (w.at[0], y.at[0]))
+                unpack(hp[side, 8 + b], side * 2 * OWN + block, w.at[0])
 
     for g in (3, 4, 7, 8, 2, 9, 1, 10):
         one(4, g)
@@ -371,7 +376,7 @@
     ro[r] = (total * SCALE).astype(BF)
 
     spread = []
-    for i in (8, 7, 9, 6, 10, 5, 11, 4, 12, 3, 13, 2, 14, 1, 15):
+    for i in (12, 11, 13, 10, 14, 4, 3, 5, 9, 15, 2, 6, 7, 8, 1):
         copy = remote(ro.at[r], ro.at[r], SPREAD + i, (lax.rem(r + i, 16), c))
         copy.start()
         spread.append(copy)

time: 68.4 us -> 64.4 us (0.942)
  Pallas kernels: 66.3 us -> 62.3 us
    pallas_call x1, Pallas kernels: 66.3 us -> 62.3 us  [per_device(): pl.pallas_call(kernel, out_shape=(jax.ShapeDtypeStruct((64, 1024), BF), j...]
where the time goes in v3:
time: 64.4 us; the launch traced here: 64.3 us
  Pallas kernels  62.3 us (97%)
  local copies, waits for them, and re-layouts  1.36 us (2%)
    pallas_call x1, Pallas kernels, per_device(): pl.pallas_call(kernel, out_shape=(jax.ShapeDtypeStruct((64, 1024), BF), j...  62.3 us
    unnamed x2, local copies, waits for them, and re-layouts  1.36 us

profile of v3, /device:TPU:1, one launch (start us, length us, event | category | flops | bytes accessed | tf_op | source)
XLA Modules:
  0.0 64.3 jit_solution(6440308630699852556)
XLA Ops:
  0.6 62.3 %filter_and_gram.1 = (bf16[64,1024]{1,0:T(8,128)(2,1)S(1)}, f32[64,1024]{1,0:T(8,128)S(1)}) custom-call(bf16[64,1024]{1,0:T(8,128)(2,1)} %x_hbm.1, s32[8,16]{1,0:T(8,128)} %bitcast.1, bf16[16,64,512]{2,1,0:T(8,128)(2,1)} %tiles_hbm.1), custom_call_target="tpu_custom_call" | custom-call | tf_op jit(solution)/shard_map/filter_and_gram/pallas_call | solution.py:406
  62.9 0.7 %copy.7 = bf16[64,1024]{1,0:T(8,128)(2,1)} copy(bf16[64,1024]{1,0:T(8,128)(2,1)S(1)} %get-tuple-element.4) | data formatting | bytes 262144
  63.6 0.7 %copy.8 = f32[64,1024]{1,0:T(8,128)} copy(f32[64,1024]{1,0:T(8,128)S(1)} %get-tuple-element.5) | data formatting | bytes 524288

commit v4 on v3

--- a/solution.py
+++ b/solution.py
@@ -15,7 +15,7 @@
 SCALE = 1.0 / 16384
 
 A2A, TIL, IDX, VEC, EARLY, OLD, LATE = 0, 16, 22, 24, 26, 28, 30
-QUART, GATH, PAIR, XRED, ZRED, SPREAD, COUNT = 32, 36, 52, 56, 60, 68, 84
+QUART, GATH, PAIR, XRED, ZRED, SPREAD, RELAY, COUNT = 32, 36, 52, 56, 72, 80, 88, 96
 
 
 def swap(v):
@@ -53,13 +53,18 @@
 
     for i in (8, 7, 9, 6, 10, 5, 11, 4, 12, 3, 13, 2, 14, 1, 15):
         greet((r, lax.rem(c + i, 16)))
-        greet((lax.rem(r + i, 16), c))
-    for i in range(1, 4):
+    for i in range(4):
         greet((lax.rem(r + 8, 16), lax.rem(zh + i, 4) * 4 + yy))
+    for i in range(1, 8):
+        greet((zl * 8 + lax.rem(r + i, 8), c))
     at_7, at_8 = r == 7, r == 8
     middle = jnp.logical_or(at_7, at_8)
     turned = jnp.where(at_7, lax.rem(zh + 3, 4), lax.rem(zh + 1, 4)) * 4 + yy
-    pl.when(middle)(lambda: greet((15 - r, turned)))
+    @pl.when(middle)
+    def _():
+        greet((15 - r, c))
+        greet((15 - r, turned))
+
     own_x.start()
     own_cols.start()
     own_tiles.start()
@@ -96,8 +101,8 @@
     idxv[...] = jnp.zeros_like(idxv)
     idxv[:, :OWN] = slabs
 
-    pl.when(middle)(lambda: pl.semaphore_wait(barrier, 34))
-    pl.when(jnp.logical_not(middle))(lambda: pl.semaphore_wait(barrier, 33))
+    pl.when(middle)(lambda: pl.semaphore_wait(barrier, 28))
+    pl.when(jnp.logical_not(middle))(lambda: pl.semaphore_wait(barrier, 26))
 
     a2a = []
     for i in (8, 7, 9, 6, 10, 5, 11, 4, 12, 3, 13, 2, 14, 1, 15):
@@ -122,14 +127,32 @@
         pl.when(has_low)(pair[1].wait_send)
 
     idx = both_sides(IDX, idxv, idxv, idxh.at[0], idxh.at[1])
+    mine_of = [th.at[side, 2, pl.ds(yy, 1)] for side in range(2)]
+    far = both_sides(
+        TIL + 4, tiles_hbm.at[pl.ds(4 + yy, 1)], tiles_hbm.at[pl.ds(8 + yy, 1)], *mine_of
+    )
     til = [
         both_sides(
             TIL + 2 * n, tiles_hbm.at[pl.ds(4 * (3 - n), 4)], tiles_hbm.at[pl.ds(4 * n, 4)],
             th.at[0, n], th.at[1, n],
             *((jnp.where(at_7, turned, c), jnp.where(at_8, turned, c)) if n == 1 else (c, c)),
         )
-        for n in range(3)
+        for n in range(2)
     ]
+    relay = [
+        [
+            remote(v, v, RELAY + 4 * side + j, (r, zh * 4 + lax.rem(yy + j, 4)))
+            for j in (2, 1, 3)
+        ]
+        for side, v in enumerate(mine_of)
+    ]
+
+    def on_side(side, method):
+        @pl.when(edges[side])
+        def _():
+            for copy in relay[side]:
+                getattr(copy, method)()
+
     xr[c] = xs[c]
 
     low_lanes = lax.broadcasted_iota(jnp.int32, (TILE, 128), 1) < 64
@@ -161,6 +184,9 @@
         return carry
 
     lax.fori_loop(0, 4, place_own, 0)
+    arrived(far)
+    for side in range(2):
+        on_side(side, "start")
 
     def unpack(v, block, ref):
         for half in range(2):
@@ -204,8 +230,11 @@
             to_smem(idxh.at[side], side)
 
     def halo_tiles(n):
-        arrived(til[n])
+        if n < 2:
+            arrived(til[n])
         for side in range(2):
+            if n == 2:
+                on_side(side, "wait_recv")
 
             @pl.when(edges[side])
             def _(side=side):
@@ -337,16 +366,21 @@
     for i in order:
         gf[i] = jnp.dot(mine, fy[core * 4 + lax.rem(x + i, 4)], preferred_element_type=F32)
 
-    xred = []
+    xred = {}
+    parts = [lax.rem(zh + d, 4) for d in (2, 1, 3, 0)]
     for i in order:
         pairs[i].wait_recv()
         total = gf[i] + gr[i].astype(F32)
         if i:
-            to = lax.rem(x + i, 4)
             xsnd[i] = total.astype(BF)
-            copy = remote(xsnd.at[i], xrcv.at[i], XRED + i, (zl * 8 + to * 2 + core, c))
-            copy.start()
-            xred.append((i, copy))
+        else:
+            gf[0] = total
+    for k, part in enumerate(parts):
+        rows = pl.ds(pl.multiple_of(part * 64, 64), 64)
+        for i in order[:3]:
+            device = (zl * 8 + lax.rem(x + i, 4) * 2 + core, c)
+            xred[i, k] = remote(xsnd.at[i, rows], xrcv.at[i, rows], XRED + 4 * i + k, device)
+            xred[i, k].start()
 
     rows = pl.ds(pl.multiple_of(yy * TILE, TILE), TILE)
     for h in range(4):
@@ -356,47 +390,52 @@
                 [fy[4 * p + h // 2, rows, lanes], fy[4 * p + 2 + h // 2, rows, lanes]], axis=1
             )
 
-    for i, copy in xred:
+    for k, part in enumerate(parts):
+        rows = pl.ds(pl.multiple_of(part * 64, 64), 64)
+        total = gf[0, rows, :]
+        for i in order[:3]:
+            xred[i, k].wait_recv()
+            total = total + xrcv[i, rows, :].astype(F32)
+        zs[rows, :] = total.astype(BF)
+        for lo in (zl, 1 - zl) if k < 3 else (1 - zl,):
+            i = lax.rem(part * 2 + lo - z + 8, 8)
+            copy = remote(zs.at[rows], zr.at[z], ZRED + i, (lo * 8 + x * 2 + core, part * 4 + yy))
+            copy.start()
+    zr[z] = zs[pl.ds(pl.multiple_of(zh * 64, 64), 64), :]
+    landed = [remote(zs.at[pl.ds(0, 64)], zr.at[z], ZRED + i, pair_dev) for i in range(1, 8)]
+    for copy in landed:
         copy.wait_recv()
-        total = total + xrcv[i].astype(F32)
-    gf[0] = total
-    zs[...] = total.astype(BF)
-
-    zred = []
-    for i in (4, 3, 5, 2, 6, 1, 7):
-        to = lax.rem(z + i, 8)
-        device = (lax.rem(to, 2) * 8 + x * 2 + core, (to // 2) * 4 + yy)
-        copy = remote(zs.at[pl.ds(pl.multiple_of(to * 32, 32), 32)], zr.at[i], ZRED + i, device)
-        copy.start()
-        zred.append((i, copy))
-    total = gf[0, pl.ds(pl.multiple_of(z * 32, 32), 32), :]
-    for i, copy in zred:
-        copy.wait_recv()
+    total = zr[0].astype(F32)
+    for i in range(1, 8):
         total = total + zr[i].astype(F32)
-    ro[r] = (total * SCALE).astype(BF)
+    rr = lax.rem(r, 8)
+    ro[rr] = (total * SCALE).astype(BF)
 
     spread = []
-    for i in (12, 11, 13, 10, 14, 4, 3, 5, 9, 15, 2, 6, 7, 8, 1):
-        copy = remote(ro.at[r], ro.at[r], SPREAD + i, (lax.rem(r + i, 16), c))
+    for i in (4, 3, 5, 2, 6, 7, 1):
+        copy = remote(ro.at[rr], ro.at[rr], SPREAD + i, (zl * 8 + lax.rem(rr + i, 8), c))
         copy.start()
         spread.append(copy)
 
-    for pair in (idx, *til, vec, old, early, late):
+    for side in range(2):
+        on_side(side, "wait_send")
+    for pair in (idx, far, *til, vec, old, early, late):
         sent(pair)
     for copy in a2a + gath:
         copy.wait_send()
-    for i, copy in quart + list(pairs.items()) + xred + zred:
+    for i, copy in quart + list(pairs.items()):
+        copy.wait_send()
+    for copy in list(xred.values()) + landed:
         copy.wait_send()
     for copy in spread:
         copy.wait_recv()
-    for l in range(2):
-        for h in range(4):
-            for p in range(2):
-                lanes = slice((h % 2) * 64, (h % 2 + 1) * 64)
-                at = [l * 8 + (k * 2 + h // 2) * 2 + p for k in range(2)]
-                gram_ref[l * 32 : (l + 1) * 32, h * 256 + p * 128 : h * 256 + (p + 1) * 128] = (
-                    jnp.concatenate([ro[at[0]][:, lanes], ro[at[1]][:, lanes]], axis=1).astype(F32)
-                )
+    for h in range(4):
+        for p in range(2):
+            lanes = slice((h % 2) * 64, (h % 2 + 1) * 64)
+            at = [(k * 2 + h // 2) * 2 + p for k in range(2)]
+            gram_ref[:, h * 256 + p * 128 : h * 256 + (p + 1) * 128] = jnp.concatenate(
+                [ro[at[0]][:, lanes], ro[at[1]][:, lanes]], axis=1
+            ).astype(F32)
     for copy in spread:
         copy.wait_send()
 
@@ -439,8 +478,8 @@
             pltpu.VMEM((4, 256, 128), BF),
             pltpu.VMEM((4, 256, 128), BF),
             pltpu.VMEM((256, 128), BF),
-            pltpu.VMEM((8, 32, 128), BF),
-            pltpu.VMEM((16, 32, 128), BF),
+            pltpu.VMEM((8, 64, 128), BF),
+            pltpu.VMEM((8, 64, 128), BF),
             pltpu.SemaphoreType.DMA((4,)),
             pltpu.SemaphoreType.DMA((COUNT,)),
             pltpu.SemaphoreType.DMA((COUNT,)),

time: 64.4 us -> 62.7 us (0.974)
  Pallas kernels: 62.3 us -> 60.6 us
    pallas_call x1, Pallas kernels: 62.3 us -> 60.6 us  [per_device(): pl.pallas_call(kernel, out_shape=(jax.ShapeDtypeStruct((64, 1024), BF), j...]
where the time goes in v4:
time: 62.7 us; the launch traced here: 62.6 us
  Pallas kernels  60.6 us (97%)
  local copies, waits for them, and re-layouts  1.36 us (2%)
  between operations  0.64 us (1%)
    pallas_call x1, Pallas kernels, per_device(): pl.pallas_call(kernel, out_shape=(jax.ShapeDtypeStruct((64, 1024), BF), j...  60.6 us
    unnamed x2, local copies, waits for them, and re-layouts  1.36 us

profile of v4, /device:TPU:1, one launch (start us, length us, event | category | flops | bytes accessed | tf_op | source)
XLA Modules:
  0.0 62.6 jit_solution(17082686103844577090)
XLA Ops:
  0.6 60.6 %filter_and_gram.1 = (bf16[64,1024]{1,0:T(8,128)(2,1)S(1)}, f32[64,1024]{1,0:T(8,128)S(1)}) custom-call(bf16[64,1024]{1,0:T(8,128)(2,1)} %x_hbm.1, s32[8,16]{1,0:T(8,128)} %bitcast.1, bf16[16,64,512]{2,1,0:T(8,128)(2,1)} %tiles_hbm.1), custom_call_target="tpu_custom_call" | custom-call | tf_op jit(solution)/shard_map/filter_and_gram/pallas_call | solution.py:445
  61.3 0.7 %copy.7 = bf16[64,1024]{1,0:T(8,128)(2,1)} copy(bf16[64,1024]{1,0:T(8,128)(2,1)S(1)} %get-tuple-element.4) | data formatting | bytes 262144
  61.9 0.7 %copy.8 = f32[64,1024]{1,0:T(8,128)} copy(f32[64,1024]{1,0:T(8,128)S(1)} %get-tuple-element.5) | data formatting | bytes 524288

commit v5 on v4

--- a/solution.py
+++ b/solution.py
@@ -28,13 +28,14 @@
 
 def kernel(
     x_hbm, cols_hbm, tiles_hbm, out_ref, gram_ref,
-    x_ref, cols_ref, xs, xr, tv, th, idxv, idxh, idxs, slab, band, hx, hp, ho, w, y,
+    x_ref, cols_ref, xs, xr, tv, th, idxv, idxh, idxs, slab, band, hx, hp, ho, w0, w1, y0, y1,
     fp, op, fq, pc, fy, gs, gr, gf, xsnd, xrcv, zs, zr, ro, local_sem, ss, rs,
 ):
     r, c = lax.axis_index("rows"), lax.axis_index("cols")
     yy, zh = lax.rem(c, 4), c // 4
     core, x, zl = lax.rem(r, 2), lax.rem(r // 2, 4), r // 8
     z = zh * 2 + zl
+    w, y = (w0, w1), (y0, y1)
 
     def remote(src, dst, number, device):
         return pltpu.make_async_remote_copy(
@@ -81,7 +82,7 @@
         @pl.when(jnp.logical_not(edges[side]))
         def _(side=side):
             zero(band, 7 * side * GROUP, 3 * GROUP)
-            zero(w.at[0], side * 8 * GROUP, 4 * GROUP)
+            zero(w[0], side * 8 * GROUP, 4 * GROUP)
 
     for u in range(4):
         slab[u, 8] = jnp.zeros((TILE, 128), BF)
@@ -193,32 +194,33 @@
             rows = pl.ds(block * TILE + half * 32, 32)
             ref[rows, :] = v[:, half * 64 : (half + 1) * 64].astype(ref.dtype)
 
-    def one(n, g):
+    def one(n, k, turn=False):
+        g = jnp.where(core == 0, k, 11 - k) if turn else k
         now, later = n % 2, (n + 1) % 2
         at = g * GROUP if isinstance(g, int) else pl.multiple_of(g * GROUP, GROUP)
         back = (g - 1) * GROUP if isinstance(g, int) else pl.multiple_of((g - 1) * GROUP, GROUP)
         rows = pl.ds(at, GROUP)
         product = jnp.dot(
-            band[pl.ds(back, GROUP), :], w[now, pl.ds(back, WIN), :], preferred_element_type=F32
+            band[pl.ds(back, GROUP), :], w[now][pl.ds(back, WIN), :], preferred_element_type=F32
         )
-        outer = n in (4, 5) and not 4 <= g <= 7
-        current = w[now, rows, :].astype(F32) if n == 0 or (n == 4 and outer) else y[now, rows, :]
+        outer = n in (4, 5) and not 4 <= k <= 7
+        current = w[now][rows, :].astype(F32) if n == 0 or (n == 4 and outer) else y[now][rows, :]
         if n == 0:
             new = (product - 0.1 * current) * 0.5
         else:
             before = w if n == 1 or (n == 5 and outer) else y
-            new = product - 0.1 * current - before[later, rows, :].astype(F32)
+            new = product - 0.1 * current - before[later][rows, :].astype(F32)
         rounded = new.astype(BF)
         if n < 7:
-            y[later, rows, :] = new
-            w[later, rows, :] = rounded
+            y[later][rows, :] = new
+            w[later][rows, :] = rounded
         return rounded
 
     for copy in a2a:
         copy.wait_recv()
     vec = both_sides(VEC, xr, xr, hx.at[0], hx.at[1])
     for b in range(OWN):
-        unpack(xr[b], OWN + b, w.at[0])
+        unpack(xr[b], OWN + b, w[0])
     for g in (5, 6):
         one(0, g)
 
@@ -229,40 +231,43 @@
         def _(side=side):
             to_smem(idxh.at[side], side)
 
-    def halo_tiles(n):
-        if n < 2:
-            arrived(til[n])
+    def on_fast(fast, work):
         for side in range(2):
-            if n == 2:
-                on_side(side, "wait_recv")
-
-            @pl.when(edges[side])
-            def _(side=side):
-                place(
-                    th.at[side, n], side, 4 * (3 - n) if side == 0 else 4 * n,
-                    (2 - n if side == 0 else 7 + n) * GROUP,
-                )
-
-    halo_tiles(0)
-    halo_tiles(1)
-
-    arrived(vec)
-    for side in range(2):
-
-        @pl.when(edges[side])
-        def _(side=side):
-            for b in range(OWN):
-                unpack(hx[side, b], side * 2 * OWN + b, w.at[0])
-
-    for g in (4, 7, 3, 8, 2, 9):
-        one(0, g)
-    for g in (5, 6, 4, 7, 3, 8):
-        one(1, g)
-    for g in (5, 6, 4, 7):
-        one(2, g)
+            here = core == (1 - side if fast else side)
+            pl.when(jnp.logical_and(here, edges[side]))(lambda side=side: work(side))
+
+    def place_chunk(side, n):
+        place(
+            th.at[side, n], side, 4 * (3 - n) if side == 0 else 4 * n,
+            (2 - n if side == 0 else 7 + n) * GROUP,
+        )
+
+    def near_chunks(side):
+        for n in range(2):
+            til[n][side].wait_recv()
+            place_chunk(side, n)
+
+    def vectors(side):
+        vec[side].wait_recv()
+        for b in range(OWN):
+            unpack(hx[side, b], side * 2 * OWN + b, w[0])
+
+    def far_chunk(side):
+        for copy in relay[side]:
+            copy.wait_recv()
+        place_chunk(side, 2)
+
+    on_fast(True, near_chunks)
+    on_fast(True, vectors)
+    for n, k in ((0, 7), (0, 8), (0, 9), (1, 6), (1, 7), (1, 8), (2, 7)):
+        one(n, k, True)
+    on_fast(False, near_chunks)
+    on_fast(False, vectors)
+    for n, k in ((0, 4), (0, 3), (0, 2), (1, 5), (1, 4), (1, 3), (2, 6), (2, 5), (2, 4)):
+        one(n, k, True)
 
     for b in range(8):
-        op[b] = pack(y[1, pl.ds((20 + b) * TILE, TILE), :]).astype(BF)
+        op[b] = pack(y[1][pl.ds((20 + b) * TILE, TILE), :]).astype(BF)
     old = both_sides(OLD, op, op, ho.at[0], ho.at[1])
 
     def pack_group(rounded, dst, first):
@@ -274,7 +279,8 @@
     early = both_sides(
         EARLY, fp.at[pl.ds(0, 8)], fp.at[pl.ds(0, 8)], hp.at[0, pl.ds(0, 8)], hp.at[1, pl.ds(0, 8)]
     )
-    halo_tiles(2)
+    on_fast(True, far_chunk)
+    on_fast(False, far_chunk)
     for n, g in ((0, 1), (0, 10), (1, 2), (1, 9), (2, 3), (2, 8)):
         one(n, g)
     for slot, g in ((8, 4), (12, 7)):
@@ -285,33 +291,25 @@
     for g in (5, 6):
         one(4, g)
 
-    arrived(old)
-    arrived(early)
-    for side in range(2):
-
-        @pl.when(edges[side])
-        def _(side=side):
-            for b in range(8):
-                unpack(hp[side, b], side * 2 * OWN + 4 + b, w.at[0])
-                unpack(ho[side, b], side * 2 * OWN + 4 + b, y.at[1])
-
-    arrived(late)
-    for side in range(2):
-
-        @pl.when(edges[side])
-        def _(side=side):
-            for b in range(8):
-                block = b if b < 4 else b + 8
-                unpack(hp[side, 8 + b], side * 2 * OWN + block, w.at[0])
-
-    for g in (3, 4, 7, 8, 2, 9, 1, 10):
-        one(4, g)
-    for g in (5, 6, 4, 7, 3, 8, 2, 9):
-        one(5, g)
-    for g in (5, 6, 4, 7, 3, 8):
-        one(6, g)
-
-    quart, gath = [], []
+    def later_vectors(side):
+        for pair in (old, early, late):
+            pair[side].wait_recv()
+        first = side * 2 * OWN
+        for b in range(8):
+            unpack(hp[side, b], first + 4 + b, w[0])
+            unpack(ho[side, b], first + 4 + b, y[1])
+            unpack(hp[side, 8 + b], first + (b if b < 4 else b + 8), w[0])
+
+    on_fast(True, later_vectors)
+    for n, ks in ((4, (7, 8, 9, 10)), (5, (6, 7, 8, 9)), (6, (7, 8))):
+        for k in ks:
+            one(n, k, True)
+    on_fast(False, later_vectors)
+    for n, ks in ((4, (4, 3, 2, 1)), (5, (5, 4, 3, 2)), (6, (6, 5, 4, 3))):
+        for k in ks:
+            one(n, k, True)
+
+    quart, gath = [], {}
     for i in (2, 1, 3, 0):
         to = lax.rem(zh + i, 4)
         rounded = one(7, 4 + to)
@@ -329,7 +327,7 @@
             device = (r, zh * 4 + lax.rem(yy + j, 4))
             copy = remote(piece, piece, GATH + 4 * i + j, device)
             copy.start()
-            gath.append(copy)
+            gath[i, j] = copy
 
     to_y(0)
     for i, copy in (quart[1], quart[2], quart[0]):
@@ -350,10 +348,10 @@
     mine = jnp.concatenate(
         [fy[2 * yy + half].astype(F32).T.astype(BF) for half in range(2)], axis=0
     )
-    for copy in gath:
-        copy.wait_recv()
-    for j in range(1, 4):
-        assemble(lax.rem(yy + j, 4))
+    for j in (1, 3, 2):
+        for i in range(4):
+            gath[i, j].wait_recv()
+        assemble(lax.rem(yy - j + 4, 4))
 
     pair_dev = (r + 1 - 2 * core, c)
     order = (2, 1, 3, 0)
@@ -421,7 +419,7 @@
         on_side(side, "wait_send")
     for pair in (idx, far, *til, vec, old, early, late):
         sent(pair)
-    for copy in a2a + gath:
+    for copy in a2a + list(gath.values()):
         copy.wait_send()
     for i, copy in quart + list(pairs.items()):
         copy.wait_send()
@@ -465,8 +463,10 @@
             pltpu.VMEM((2, 16, 32, 128), BF),
             pltpu.VMEM((2, 16, 32, 128), BF),
             pltpu.VMEM((2, 8, 32, 128), BF),
-            pltpu.VMEM((2, ext, 64), BF),
-            pltpu.VMEM((2, ext, 64), F32),
+            pltpu.VMEM((ext, 64), BF),
+            pltpu.VMEM((ext, 64), BF),
+            pltpu.VMEM((ext, 64), F32),
+            pltpu.VMEM((ext, 64), F32),
             pltpu.VMEM((16, 32, 128), BF),
             pltpu.VMEM((8, 32, 128), BF),
             pltpu.VMEM((4, 4, 32, 128), BF),

time: 62.7 us -> 61.8 us (0.986)
  Pallas kernels: 60.6 us -> 59.7 us
    pallas_call x1, Pallas kernels: 60.6 us -> 59.7 us  [per_device(): pl.pallas_call(kernel, out_shape=(jax.ShapeDtypeStruct((64, 1024), BF), j...]
where the time goes in v5:
time: 61.8 us; the launch traced here: 61.7 us
  Pallas kernels  59.7 us (97%)
  local copies, waits for them, and re-layouts  1.36 us (2%)
  between operations  0.64 us (1%)
    pallas_call x1, Pallas kernels, per_device(): pl.pallas_call(kernel, out_shape=(jax.ShapeDtypeStruct((64, 1024), BF), j...  59.7 us
    unnamed x2, local copies, waits for them, and re-layouts  1.36 us

profile of v5, /device:TPU:1, one launch (start us, length us, event | category | flops | bytes accessed | tf_op | source)
XLA Modules:
  0.0 61.7 jit_solution(2558223836963088658)
XLA Ops:
  0.6 59.7 %filter_and_gram.1 = (bf16[64,1024]{1,0:T(8,128)(2,1)S(1)}, f32[64,1024]{1,0:T(8,128)S(1)}) custom-call(bf16[64,1024]{1,0:T(8,128)(2,1)} %x_hbm.1, s32[8,16]{1,0:T(8,128)} %bitcast.1, bf16[16,64,512]{2,1,0:T(8,128)(2,1)} %tiles_hbm.1), custom_call_target="tpu_custom_call" | custom-call | tf_op jit(solution)/shard_map/filter_and_gram/pallas_call | solution.py:443
  60.3 0.7 %copy.7 = bf16[64,1024]{1,0:T(8,128)(2,1)} copy(bf16[64,1024]{1,0:T(8,128)(2,1)S(1)} %get-tuple-element.4) | data formatting | bytes 262144
  61.0 0.7 %copy.8 = f32[64,1024]{1,0:T(8,128)} copy(f32[64,1024]{1,0:T(8,128)S(1)} %get-tuple-element.5) | data formatting | bytes 524288

commit v6 on v5

--- a/solution.py
+++ b/solution.py
@@ -128,10 +128,28 @@
         pl.when(has_low)(pair[1].wait_send)
 
     idx = both_sides(IDX, idxv, idxv, idxh.at[0], idxh.at[1])
+    def on_fast(fast, work):
+        for side in range(2):
+            here = core == (1 - side if fast else side)
+            pl.when(jnp.logical_and(here, edges[side]))(lambda side=side: work(side))
+
     mine_of = [th.at[side, 2, pl.ds(yy, 1)] for side in range(2)]
-    far = both_sides(
-        TIL + 4, tiles_hbm.at[pl.ds(4 + yy, 1)], tiles_hbm.at[pl.ds(8 + yy, 1)], *mine_of
+    whole = (
+        remote(tiles_hbm.at[pl.ds(4, 4)], th.at[0, 2], TIL + 4, (up, c)),
+        remote(tiles_hbm.at[pl.ds(8, 4)], th.at[1, 2], TIL + 5, (down, c)),
     )
+    shared = (
+        remote(tiles_hbm.at[pl.ds(4 + yy, 1)], mine_of[0], TIL + 4, (up, c)),
+        remote(tiles_hbm.at[pl.ds(8 + yy, 1)], mine_of[1], TIL + 5, (down, c)),
+    )
+
+    def far_out(method):
+        pl.when(jnp.logical_and(core == 1, has_high))(lambda: getattr(shared[0], method)())
+        pl.when(jnp.logical_and(core == 0, has_low))(lambda: getattr(shared[1], method)())
+        pl.when(core == 0)(lambda: getattr(whole[0], method)())
+        pl.when(core == 1)(lambda: getattr(whole[1], method)())
+
+    far_out("start")
     til = [
         both_sides(
             TIL + 2 * n, tiles_hbm.at[pl.ds(4 * (3 - n), 4)], tiles_hbm.at[pl.ds(4 * n, 4)],
@@ -148,12 +166,6 @@
         for side, v in enumerate(mine_of)
     ]
 
-    def on_side(side, method):
-        @pl.when(edges[side])
-        def _():
-            for copy in relay[side]:
-                getattr(copy, method)()
-
     xr[c] = xs[c]
 
     low_lanes = lax.broadcasted_iota(jnp.int32, (TILE, 128), 1) < 64
@@ -185,9 +197,13 @@
         return carry
 
     lax.fori_loop(0, 4, place_own, 0)
-    arrived(far)
-    for side in range(2):
-        on_side(side, "start")
+
+    def pass_on(side):
+        shared[side].wait_recv()
+        for copy in relay[side]:
+            copy.start()
+
+    on_fast(False, pass_on)
 
     def unpack(v, block, ref):
         for half in range(2):
@@ -231,11 +247,6 @@
         def _(side=side):
             to_smem(idxh.at[side], side)
 
-    def on_fast(fast, work):
-        for side in range(2):
-            here = core == (1 - side if fast else side)
-            pl.when(jnp.logical_and(here, edges[side]))(lambda side=side: work(side))
-
     def place_chunk(side, n):
         place(
             th.at[side, n], side, 4 * (3 - n) if side == 0 else 4 * n,
@@ -252,12 +263,17 @@
         for b in range(OWN):
             unpack(hx[side, b], side * 2 * OWN + b, w[0])
 
+    def far_chunk_here(side):
+        whole[side].wait_recv()
+        place_chunk(side, 2)
+
     def far_chunk(side):
         for copy in relay[side]:
             copy.wait_recv()
         place_chunk(side, 2)
 
     on_fast(True, near_chunks)
+    on_fast(True, far_chunk_here)
     on_fast(True, vectors)
     for n, k in ((0, 7), (0, 8), (0, 9), (1, 6), (1, 7), (1, 8), (2, 7)):
         one(n, k, True)
@@ -279,7 +295,6 @@
     early = both_sides(
         EARLY, fp.at[pl.ds(0, 8)], fp.at[pl.ds(0, 8)], hp.at[0, pl.ds(0, 8)], hp.at[1, pl.ds(0, 8)]
     )
-    on_fast(True, far_chunk)
     on_fast(False, far_chunk)
     for n, g in ((0, 1), (0, 10), (1, 2), (1, 9), (2, 3), (2, 8)):
         one(n, g)
@@ -415,9 +430,13 @@
         copy.start()
         spread.append(copy)
 
-    for side in range(2):
-        on_side(side, "wait_send")
-    for pair in (idx, far, *til, vec, old, early, late):
+    def passed_on(side):
+        for copy in relay[side]:
+            copy.wait_send()
+
+    on_fast(False, passed_on)
+    far_out("wait_send")
+    for pair in (idx, *til, vec, old, early, late):
         sent(pair)
     for copy in a2a + list(gath.values()):
         copy.wait_send()

time: 61.8 us -> 61.5 us (level)
  no operation moved by 1% of the time
where the time goes in v6:
time: 61.5 us; the launch traced here: 61.4 us
  Pallas kernels  59.4 us (97%)
  local copies, waits for them, and re-layouts  1.36 us (2%)
  between operations  0.64 us (1%)
    pallas_call x1, Pallas kernels, per_device(): pl.pallas_call(kernel, out_shape=(jax.ShapeDtypeStruct((64, 1024), BF), j...  59.4 us
    unnamed x2, local copies, waits for them, and re-layouts  1.36 us

profile of v6, /device:TPU:1, one launch (start us, length us, event | category | flops | bytes accessed | tf_op | source)
XLA Modules:
  0.0 61.4 jit_solution(4292210217782472535)
XLA Ops:
  0.6 59.4 %filter_and_gram.1 = (bf16[64,1024]{1,0:T(8,128)(2,1)S(1)}, f32[64,1024]{1,0:T(8,128)S(1)}) custom-call(bf16[64,1024]{1,0:T(8,128)(2,1)} %x_hbm.1, s32[8,16]{1,0:T(8,128)} %bitcast.1, bf16[16,64,512]{2,1,0:T(8,128)(2,1)} %tiles_hbm.1), custom_call_target="tpu_custom_call" | custom-call | tf_op jit(solution)/shard_map/filter_and_gram/pallas_call | solution.py:462
  60.1 0.7 %copy.7 = bf16[64,1024]{1,0:T(8,128)(2,1)} copy(bf16[64,1024]{1,0:T(8,128)(2,1)S(1)} %get-tuple-element.4) | data formatting | bytes 262144
  60.7 0.7 %copy.8 = f32[64,1024]{1,0:T(8,128)} copy(f32[64,1024]{1,0:T(8,128)S(1)} %get-tuple-element.5) | data formatting | bytes 524288

commit v7 on v6

--- a/solution.py
+++ b/solution.py
@@ -204,6 +204,13 @@
             copy.start()
 
     on_fast(False, pass_on)
+
+    arrived(idx)
+    for side in range(2):
+
+        @pl.when(edges[side])
+        def _(side=side):
+            to_smem(idxh.at[side], side)
 
     def unpack(v, block, ref):
         for half in range(2):
@@ -239,13 +246,6 @@
         unpack(xr[b], OWN + b, w[0])
     for g in (5, 6):
         one(0, g)
-
-    arrived(idx)
-    for side in range(2):
-
-        @pl.when(edges[side])
-        def _(side=side):
-            to_smem(idxh.at[side], side)
 
     def place_chunk(side, n):
         place(

time: 61.5 us -> 62 us (level)
  no operation moved by 1% of the time
where the time goes in v7:
time: 62 us; the launch traced here: 61.9 us
  Pallas kernels  59.9 us (97%)
  local copies, waits for them, and re-layouts  1.36 us (2%)
  between operations  0.64 us (1%)
    pallas_call x1, Pallas kernels, per_device(): pl.pallas_call(kernel, out_shape=(jax.ShapeDtypeStruct((64, 1024), BF), j...  59.9 us
    unnamed x2, local copies, waits for them, and re-layouts  1.36 us

profile of v7, /device:TPU:1, one launch (start us, length us, event | category | flops | bytes accessed | tf_op | source)
XLA Modules:
  0.0 61.9 jit_solution(15481789941076035980)
XLA Ops:
  0.6 59.9 %filter_and_gram.1 = (bf16[64,1024]{1,0:T(8,128)(2,1)S(1)}, f32[64,1024]{1,0:T(8,128)S(1)}) custom-call(bf16[64,1024]{1,0:T(8,128)(2,1)} %x_hbm.1, s32[8,16]{1,0:T(8,128)} %bitcast.1, bf16[16,64,512]{2,1,0:T(8,128)(2,1)} %tiles_hbm.1), custom_call_target="tpu_custom_call" | custom-call | tf_op jit(solution)/shard_map/filter_and_gram/pallas_call | solution.py:462
  60.5 0.7 %copy.7 = bf16[64,1024]{1,0:T(8,128)(2,1)} copy(bf16[64,1024]{1,0:T(8,128)(2,1)S(1)} %get-tuple-element.4) | data formatting | bytes 262144
  61.2 0.7 %copy.8 = f32[64,1024]{1,0:T(8,128)} copy(f32[64,1024]{1,0:T(8,128)S(1)} %get-tuple-element.5) | data formatting | bytes 524288
